TPU v7x, 256 devices: a whole 4x4x8 slice. The times are simulated.
256 devices in a mesh: rows: 16 (over y_lo, z), blk: 16 (over x, y_hi, core).
Axes of the slice: x: 4, y: 4 (y_hi: 2, y_lo: 2; y = y_hi * 2 + y_lo), z: 8, core: 2. Of those that a mesh axis runs over, the one named last changes fastest.
Arguments:
- hidden: bfloat16 [262144, 256], P(('rows', 'blk')), may hold values from -6 to 6
- weight: bfloat16 [256, 256], replicated, may hold values from -0.375 to 0.375
- adjacency: bfloat16 [8192, 128, 128], P(('rows', 'blk')), may hold values from -0.3125 to 0.3125
- tile_target: int32 [8192], P(('rows', 'blk')), may hold values from 0 to 128, as said below
- tile_source: int32 [8192], P(('rows', 'blk')), may hold values from 0 to 128, as said below
- upstream: bfloat16 [262144, 256], P(('rows', 'blk')), may hold values from -6 to 6
- labels: int32 [262144], P(('rows', 'blk')), may hold values 0 or 1
Outputs:
- output: bfloat16 [262144, 256], P(('rows', 'blk'))
- d_hidden: bfloat16 [262144, 256], P(('rows', 'blk'))
- d_weight: float32 [256, 256], replicated
Inputs may be any that keep to these rules, and one draw needn't show every extreme that they name: The value 16 * 8 marks an empty slot, and exactly the same slots are empty in tile_source. Every device uses between 16 and 32 slots, some device uses all 32 and some device exactly 16. Of one device's used slots at most 2 have the same tile_target // 8, and some device reaches 2. The same pair of indices may occur in several slots. `tile_source`: the value 16 * 8 marks an empty slot, exactly where tile_target is 128.
All inputs are finite; a program needn't handle non-finite values. No bound on the sum of `labels` on one device may be relied on, other than what follows from the above.
Results may differ from a plain program's by a relative error of at most 0.02.
Values may be sent and summed in bfloat16 or wider, within the bound.
No kernel may reach another device: no remote copies, remote signals or barrier semaphores. Data moves between devices by JAX's collectives and lax.ppermute only.
A program may use at most 128 MiB of HBM per device.

v0:
```python
import math

import jax
import jax.numpy as jnp
from jax import lax
from jax.experimental import pallas as pl
from jax.experimental.pallas import tpu as pltpu
from jax.sharding import PartitionSpec as P

BF16 = jnp.bfloat16
F32 = jnp.float32
CHUNKS = 2
NOTE = 16
GROUP = 4
SMEM_SPEC = pl.BlockSpec(memory_space=pltpu.SMEM)
VMEM_SPEC = pl.BlockSpec(memory_space=pltpu.VMEM)
ANY_SPEC = pl.BlockSpec(memory_space=pl.ANY)
HBM_SPEC = pl.BlockSpec(memory_space=pltpu.HBM)
MIB = 1024 * 1024
SMALL = pltpu.CompilerParams(vmem_limit_bytes=20 * MIB)
MIDDLE = pltpu.CompilerParams(vmem_limit_bytes=44 * MIB)
LARGE = pltpu.CompilerParams(vmem_limit_bytes=56 * MIB)


def after(value, *others):
    return lax.optimization_barrier((value, *others))[0]


def blk_pairs(blk_count, dx, dy, dc):
    x_count = blk_count // 4
    pairs = []
    for b in range(blk_count):
        x, y, c = b // 4, (b // 2) % 2, b % 2
        pairs.append((b, ((x + dx) % x_count) * 4 + ((y + dy) % 2) * 2 + (c + dc) % 2))
    return pairs


def run_all(copies):
    for copy in copies:
        copy.start()
    for copy in copies:
        copy.wait()


def forward_kernel(slot_ref, source_ref, local_ref, tiles_ref, *refs):
    shards, out_ref, (held, tiles, laid, sems, out_sems) = refs[:-6], refs[-6], refs[-5:]
    rows = held.shape[1]
    copies = [pltpu.make_async_copy(tiles_ref, tiles, sems.at[0])]
    side = len(shards) // 2
    for core in range(2):
        own, across, twice, across_twice, plus, minus = shards[core * side : (core + 1) * side]
        parts = [
            own, plus.at[pl.ds(0, rows)], twice, minus.at[pl.ds(0, rows)],
            across, plus.at[pl.ds(rows, rows)],
            across_twice, minus.at[pl.ds(rows, rows)],
        ]
        for part in parts:
            place = len(copies) - 1
            copies.append(pltpu.make_async_copy(part, held.at[place], sems.at[place + 1]))
    run_all(copies)
    block = tiles.shape[1]
    noted = out_ref.shape[1] > 2 * block
    row = lax.broadcasted_iota(jnp.int32, (NOTE, out_ref.shape[2]), 0)
    stores = []
    for p in range(out_ref.shape[0]):
        for j in range(2):
            slot = jnp.maximum(slot_ref[2 * p + j], 0)
            source = jnp.maximum(source_ref[2 * p + j], 0)
            panel = held[source // 8, pl.ds(pl.multiple_of((source % 8) * block, block), block), :]
            product = jnp.dot(tiles[slot], panel, preferred_element_type=F32)
            laid[p, j * block : (j + 1) * block, :] = product.astype(BF16)
        if noted:
            note = jnp.where(row == 0, local_ref[2 * p], local_ref[2 * p + 1])
            laid[p, 2 * block :, :] = note.astype(F32).astype(BF16)
        stores.append(pltpu.make_async_copy(laid.at[p], out_ref.at[p], out_sems.at[p]))
        stores[-1].start()
    for store in stores:
        store.wait()


def sum_terms(local_ref, term_ref, total, block):
    total[...] = jnp.zeros(total.shape, F32)

    def add(p, carry):
        for j in range(2):
            local = local_ref[2 * p + j]

            @pl.when(local >= 0)
            def _():
                rows = pl.ds(pl.multiple_of(local * block, block), block)
                total[rows, :] += term_ref[p, j * block : (j + 1) * block, :].astype(F32)

        return carry

    lax.fori_loop(0, term_ref.shape[0], add, 0)


def sum_kernel(block, local_ref, term_ref, out_ref, total):
    sum_terms(local_ref, term_ref, total, block)
    out_ref[...] = total[...].astype(BF16)


def owner_kernel(block, local_ref, term_ref, *refs):
    early, (weight_ref, up_ref, sum_ref, grad_ref, send_ref) = refs[: CHUNKS - 1], refs[CHUNKS - 1 : CHUNKS + 4]
    total, weight, up, last, grad, sems, send_sems = refs[CHUNKS + 4 :]
    loads = [
        pltpu.make_async_copy(weight_ref, weight, sems.at[0]),
        pltpu.make_async_copy(up_ref, up, sems.at[1]),
    ]
    for load in loads:
        load.start()
    total[...] = jnp.zeros(total.shape, F32)
    sum_terms(local_ref, term_ref, total, block)
    for load in loads:
        load.wait()
    for g in range(total.shape[0] // block):
        rows = slice(g * block, (g + 1) * block)
        last[rows, :] = total[rows, :].astype(BF16)
        summed = jnp.dot(
            jnp.concatenate([ref[rows, :] for ref in early] + [last[rows, :]], axis=1),
            weight[...],
            preferred_element_type=F32,
        )
        logistic = jax.nn.sigmoid(summed)
        slope = logistic * (1.0 + summed * (1.0 - logistic))
        grad[rows, :] = (up[rows, :].astype(F32) * slope).astype(BF16)
    width = send_ref.shape[2]
    stores = []
    for s in range(2 * send_ref.shape[0]):
        local = jnp.maximum(local_ref[s], 0)
        rows = pl.ds(pl.multiple_of(local * block, block), block)
        stores.append(
            pltpu.make_async_copy(
                grad.at[rows, pl.ds(0, width)],
                send_ref.at[s // 2, pl.ds(s % 2 * block, block)],
                send_sems.at[s],
            )
        )
    stores.append(pltpu.make_async_copy(last, sum_ref, sems.at[2]))
    stores.append(pltpu.make_async_copy(grad, grad_ref, sems.at[3]))
    run_all(stores)


def lay_out(local_ref, grad_ref, send_ref, chunk, block):
    width = send_ref.shape[2]
    cols = slice(chunk * width, (chunk + 1) * width)
    for p in range(send_ref.shape[0]):
        for j in range(2):
            local = jnp.maximum(local_ref[2 * p + j], 0)
            rows = pl.ds(pl.multiple_of(local * block, block), block)
            send_ref[p, j * block : (j + 1) * block, :] = grad_ref[rows, cols]


def finish_kernel(block, local_ref, *refs):
    parts, (grad_ref, weight_ref, out_ref), (*send_refs, dw_ref) = (
        refs[:CHUNKS],
        refs[CHUNKS : CHUNKS + 3],
        refs[CHUNKS + 3 :],
    )
    for k, send_ref in enumerate(send_refs):
        lay_out(local_ref, grad_ref, send_ref, k + 1, block)
    weight = weight_ref[...]
    dw = jnp.zeros(dw_ref.shape, F32)
    for g in range(out_ref.shape[0] // block):
        rows = slice(g * block, (g + 1) * block)
        aggregated = jnp.concatenate([ref[rows, :] for ref in parts], axis=1)
        summed = jnp.dot(aggregated, weight, preferred_element_type=F32)
        out_ref[rows, :] = (summed * jax.nn.sigmoid(summed)).astype(BF16)
        dw = dw + lax.dot_general(
            aggregated, grad_ref[rows, :], (((0,), (0,)), ((), ())), preferred_element_type=F32
        )
    dw_ref[...] = dw


def backward_kernel(block, *refs):
    lists, (near_tiles, far_tiles, near, far), outs = refs[:8], refs[8:12], refs[12:18]
    held, laid, sems = refs[18:]
    held[...] = jnp.zeros(held.shape, F32)
    for (count_ref, tile_ref, grad_ref, place_ref), tiles, grads in (
        (lists[:4], near_tiles, near),
        (lists[4:], far_tiles, far),
    ):

        def group(i, carry):
            entries = [i * GROUP + u for u in range(GROUP)]
            products = [
                jnp.dot(
                    tiles[tile_ref[e]],
                    grads[grad_ref[e] // 2, pl.ds(pl.multiple_of(grad_ref[e] % 2 * block, block), block), :],
                    preferred_element_type=F32,
                )
                for e in entries
            ]
            for e, product in zip(entries, products):
                held[pl.ds(pl.multiple_of(place_ref[e] * block, block), block), :] += product
            return carry

        lax.fori_loop(0, (count_ref[0] + GROUP - 1) // GROUP, group, 0)
    own, across, twice, across_twice, plus, minus = outs
    rows = own.shape[0]
    order = [
        own, plus.at[pl.ds(0, rows)], twice, minus.at[pl.ds(0, rows)],
        across, plus.at[pl.ds(rows, rows)], across_twice, minus.at[pl.ds(rows, rows)],
    ]
    stores = []
    for k, out in enumerate(order):
        laid[k] = held[k * rows : (k + 1) * rows, :].astype(BF16)
        stores.append(pltpu.make_async_copy(laid.at[k], out, sems.at[k]))
        stores[-1].start()
    for store in stores:
        store.wait()


def body(hidden, weight, adjacency, tile_target, tile_source, upstream, labels):
    block = adjacency.shape[1]
    slots = adjacency.shape[0]
    own_rows, width = hidden.shape
    own_blocks = own_rows // block
    row_count = lax.axis_size("rows")
    blk_count = lax.axis_size("blk")
    share = width // CHUNKS
    me = lax.axis_index("blk")
    columns = [slice(k * share, (k + 1) * share) for k in range(CHUNKS)]

    def move(value, dx, dy, dc):
        return lax.ppermute(value, "blk", blk_pairs(blk_count, dx, dy, dc))

    order = jnp.arange(slots, dtype=jnp.int32)
    peer = tile_target // own_blocks
    earlier = (peer[:, None] == peer[None, :]) & (order[None, :] < order[:, None])
    rank = jnp.sum(earlier.astype(jnp.int32), axis=1)
    spot = jnp.where(peer < row_count, peer * 2 + rank, -1)
    at = (spot[:, None] == order[None, :]).astype(jnp.int32)
    slot_at = jnp.sum(at * (order[:, None] + 1), axis=0) - 1
    local_at = jnp.sum(at * (tile_target[:, None] % own_blocks + 1), axis=0) - 1
    source_at = jnp.sum(at * (tile_source[:, None] + 1), axis=0) - 1
    holder = source_at // own_blocks
    dx = (holder // 4 - me // 4) % 4
    dy = (holder // 2 - me // 2) % 2
    dc = (holder - me) % 2
    inner = (dy * 4 + dx) * own_blocks + source_at % own_blocks
    places = 8 * own_blocks
    panel_at = jnp.where(source_at >= 0, dc * places + inner, -1)
    near_place = jnp.where((source_at >= 0) & (dc == 0), inner, places)
    cross_place = jnp.where((source_at >= 0) & (dc == 1), inner, places)

    def side_list(slot, place):
        used = (place < places).astype(jnp.int32)
        before = (order[None, :] < order[:, None]).astype(jnp.int32)
        used_before = jnp.sum(before * used[None, :], axis=1)
        count = jnp.sum(used).reshape(1)
        position = jnp.where(used > 0, used_before, count + order - used_before)
        chosen = (position[:, None] == order[None, :]).astype(jnp.int32)
        values = (jnp.maximum(slot, 0), order, place)
        return [count] + [jnp.sum(chosen * value[:, None], axis=0) for value in values]

    far = move(jnp.stack([slot_at, cross_place]), 0, 0, 1)
    lists = side_list(slot_at, near_place) + side_list(far[0], far[1])

    turned = jnp.swapaxes(adjacency, 1, 2)
    far_turned = move(turned, 0, 0, 1)
    marked = after(
        upstream * labels.astype(BF16)[:, None], turned, far_turned, *lists
    )

    def forward(shards, note):
        return pl.pallas_call(
            forward_kernel,
            out_shape=jax.ShapeDtypeStruct((row_count, 2 * block + note, share), BF16),
            in_specs=[SMEM_SPEC] * 3 + [ANY_SPEC] * (1 + len(shards)),
            out_specs=HBM_SPEC,
            scratch_shapes=[
                pltpu.VMEM((blk_count, own_rows, share), BF16),
                pltpu.VMEM(adjacency.shape, BF16),
                pltpu.VMEM((row_count, 2 * block + note, share), BF16),
                pltpu.SemaphoreType.DMA((blk_count + 1,)),
                pltpu.SemaphoreType.DMA((row_count,)),
            ],
            compiler_params=SMALL,
            cost_estimate=pl.CostEstimate(
                flops=2 * slots * block * block * share,
                bytes_accessed=2 * own_rows * blk_count * share,
                transcendentals=0,
            ),
        )(slot_at, panel_at, local_at, adjacency, *shards)

    def exchange(value):
        return lax.all_to_all(value, "rows", 0, 0, tiled=True)

    def spread(pair):
        return [move(pair, -1, 0, 0), move(pair, 1, 0, 0)]

    def both_cores(near, *others):
        held = near[:-1] + [after(near[-1], *others)]
        return near + [move(value, 0, 0, 1) for value in held]

    own = hidden[:, columns[0]]
    twice, across = move(own, 2, 0, 0), move(own, 0, 1, 0)
    pair = after(jnp.concatenate([own, across]), twice, slot_at, panel_at, local_at)
    pairs = spread(pair)
    near = [own, across, twice, move(twice, 0, 1, 0), *pairs]
    own = after(hidden[:, columns[1]], twice, across)
    across = move(own, 0, 1, 0)
    sums = forward(both_cores(near, across), NOTE)
    twice = move(after(own, *pairs), 2, 0, 0)
    got = [exchange(sums)]
    pairs = spread(after(jnp.concatenate([own, across]), sums, twice))
    near = [own, across, twice, move(twice, 0, 1, 0), *pairs]
    got.append(exchange(forward(both_cores(near), 0)))
    local_got = got[0][:, 2 * block : 2 * block + 2, 0].astype(jnp.int32).reshape(-1)

    early = [
        pl.pallas_call(
            lambda *refs: sum_kernel(block, *refs),
            out_shape=jax.ShapeDtypeStruct((own_rows, share), BF16),
            in_specs=[SMEM_SPEC, VMEM_SPEC],
            out_specs=VMEM_SPEC,
            scratch_shapes=[pltpu.VMEM((own_rows, share), F32)],
            compiler_params=SMALL,
            cost_estimate=pl.CostEstimate(
                flops=slots * block * share, bytes_accessed=2 * slots * block * share, transcendentals=0
            ),
        )(local_got, term)
        for term in got[:-1]
    ]
    last_sums, grad, send = pl.pallas_call(
        lambda *refs: owner_kernel(block, *refs),
        out_shape=(
            jax.ShapeDtypeStruct((own_rows, share), BF16),
            jax.ShapeDtypeStruct((own_rows, width), BF16),
            jax.ShapeDtypeStruct((row_count, 2 * block, share), BF16),
        ),
        in_specs=[SMEM_SPEC] + [VMEM_SPEC] * CHUNKS + [ANY_SPEC] * 2,
        out_specs=(HBM_SPEC,) * 3,
        scratch_shapes=[
            pltpu.VMEM((own_rows, share), F32),
            pltpu.VMEM((width, width), BF16),
            pltpu.VMEM((own_rows, width), BF16),
            pltpu.VMEM((own_rows, share), BF16),
            pltpu.VMEM((own_rows, width), BF16),
            pltpu.SemaphoreType.DMA((4,)),
            pltpu.SemaphoreType.DMA((slots,)),
        ],
        compiler_params=LARGE,
        cost_estimate=pl.CostEstimate(
            flops=2 * own_rows * width * width,
            bytes_accessed=10 * own_rows * width,
            transcendentals=own_rows * width,
        ),
    )(local_got, got[-1], *early, weight, marked)
    back = [exchange(send)]
    tail_rows = width // blk_count * CHUNKS
    output, *sends, local_grad = pl.pallas_call(
        lambda *refs: finish_kernel(block, *refs),
        out_shape=(
            jax.ShapeDtypeStruct((own_rows, width), BF16),
            *[
                jax.ShapeDtypeStruct((row_count, 2 * block + tail, share), BF16)
                for tail in [0] * (CHUNKS - 2) + [tail_rows]
            ],
            jax.ShapeDtypeStruct((width, width), F32),
        ),
        in_specs=[SMEM_SPEC] + [VMEM_SPEC] * (CHUNKS + 2),
        out_specs=(VMEM_SPEC,) * (CHUNKS + 1),
        compiler_params=LARGE,
        cost_estimate=pl.CostEstimate(
            flops=4 * own_rows * width * width,
            bytes_accessed=8 * own_rows * width,
            transcendentals=own_rows * width,
        ),
    )(local_got, *early, last_sums, grad, weight)

    def backward(near):
        far_near = move(near[:, : 2 * block, :], 0, 0, 1)
        return pl.pallas_call(
            lambda *refs: backward_kernel(block, *refs),
            out_shape=[
                jax.ShapeDtypeStruct((count * own_rows, share), BF16) for count in (1, 1, 1, 1, 2, 2)
            ],
            in_specs=[SMEM_SPEC] * 8 + [VMEM_SPEC] * 4,
            out_specs=[HBM_SPEC] * 6,
            scratch_shapes=[
                pltpu.VMEM(((places + 1) * block, share), F32),
                pltpu.VMEM((8, own_rows, share), BF16),
                pltpu.SemaphoreType.DMA((8,)),
            ],
            compiler_params=MIDDLE,
            cost_estimate=pl.CostEstimate(
                flops=2 * slots * block * block * share,
                bytes_accessed=2 * own_rows * blk_count * share,
                transcendentals=0,
            ),
        )(*lists, turned, far_turned, near, far_near)

    def wide_sum(*values):
        return sum(value.astype(F32) for value in values).astype(BF16)

    def first_sums(parts):
        own, across, twice, across_twice, plus, minus = parts
        from_minus, from_plus = move(plus, 1, 0, 0), move(minus, -1, 0, 0)
        twice = wide_sum(twice, move(across_twice, 0, 1, 0))
        own = wide_sum(own, from_minus[:own_rows], from_plus[:own_rows])
        across = wide_sum(across, from_minus[own_rows:], from_plus[own_rows:])
        return [own, across, twice]

    def last_moves(parts):
        own, across, twice = parts
        return [own, move(across, 0, 1, 0), move(twice, 2, 0, 0)]

    x, y, c = me // 4, (me // 2) % 2, me % 2

    def halve(value, bit, dy, dc):
        half = value.shape[0] // 2
        keep = lax.dynamic_slice_in_dim(value, bit * half, half)
        return keep + move(lax.dynamic_slice_in_dim(value, (1 - bit) * half, half), 0, dy, dc)

    value = halve(halve(local_grad, c, 0, 1), y, 1, 0)
    rows = value.shape[0] // 4
    terms = [lax.dynamic_slice_in_dim(value, ((x + step) % 4) * rows, rows) for step in range(4)]
    piece = terms[0] + sum(move(terms[step], step, 0, 0) for step in (1, 2, 3))
    piece = jnp.concatenate([piece[:, cols] for cols in columns]).astype(BF16)
    sends[-1] = sends[-1].at[:, 2 * block :, :].set(piece[None])

    back.append(exchange(after(sends[-1], back[0])))
    piece = jnp.sum(back[-1][:, 2 * block :, :].astype(F32), axis=0)
    half_way = first_sums(backward(back[0]))
    last = backward(after(back[1], *half_way))
    received = last_moves(half_way)
    last_half_way = first_sums(after(tuple(last), *received))
    d_proj = [wide_sum(*received), wide_sum(*last_moves(last_half_way))]
    d_hidden = sum(
        lax.dot_general(
            part, weight[:, cols], (((1,), (1,)), ((), ())), preferred_element_type=F32
        )
        for part, cols in zip(d_proj, columns)
    ).astype(BF16)

    pieces = lax.all_to_all(
        jnp.broadcast_to(piece[None], (blk_count, *piece.shape)), "blk", 0, 0, tiled=True
    )
    pieces = pieces.reshape(4, 2, 2, CHUNKS, rows, share).transpose(2, 1, 0, 4, 3, 5)
    node_total = own_rows * row_count * blk_count
    d_weight = pieces.reshape(width, width) * (1.0 / math.sqrt(node_total))
    return (output, d_hidden, d_weight)


def solution(mesh):
    both = ("rows", "blk")
    return jax.shard_map(
        body,
        mesh=mesh,
        in_specs=(P(both, None), P(), P(both, None, None), P(both), P(both), P(both, None), P(both)),
        out_specs=(P(both, None), P(both, None), P()),
        check_vma=False,
    )
```

profile of v0, /device:TPU:6, one launch (start us, length us, event | category | flops | bytes accessed | tf_op | source)
XLA Modules:
  0.0 226.0 jit_solution(10142376315786384942)
XLA Ops:
  0.6 1.2 fusion.25
  1.8 3.3 %collective-permute-start = (bf16[1024,128]{1,0:T(8,128)(2,1)S(1)}, bf16[1024,128]{1,0:T(8,128)(2,1)S(1)}, u32[]{:S(2)}, u32[]{:S(2)}) collective-permute-start(bf16[1024,128]{1,0:T(8,128)(2,1)S(1)} %get-tuple-element.95.refs_0_), channel_id=1, source_target_pairs={{0,2},{1,3},{2,0},{3,1},{4,6},{5,7},{6,4},{7,5},{8,10},{9,11},{10,... | collective-permute-start | bytes 786440 | tf_op jit(solution)/shard_map/ppermute | solution.py:226
  5.1 1.4 collective-permute-start.1
  8.2 3.3 %collective-permute-done.refs_1_ = bf16[1024,128]{1,0:T(8,128)(2,1)S(1)} collective-permute-done((bf16[1024,128]{1,0:T(8,128)(2,1)S(1)}, bf16[1024,128]{1,0:T(8,128)(2,1)S(1)}, u32[]{:S(2)}, u32[]{:S(2)}) %collective-permute-start) | collective-permute-done | bytes 262176 | tf_op jit(solution)/shard_map/ppermute | solution.py:226
  11.5 2.9 %collective-permute-done.1.refs_2_ = bf16[1024,128]{1,0:T(8,128)(2,1)S(1)} collective-permute-done((bf16[1024,128]{1,0:T(8,128)(2,1)S(1)}, bf16[1024,128]{1,0:T(8,128)(2,1)S(1)}, u32[]{:S(2)}, u32[]{:S(2)}) %collective-permute-start.1) | collective-permute-done | bytes 262176 | tf_op jit(solution)/shard_map/ppermute | solution.py:226
  14.8 1.5 collective-permute-start.3
  16.8 3.1 %collective-permute-start.2 = (bf16[1024,128]{1,0:T(8,128)(2,1)S(1)}, bf16[1024,128]{1,0:T(8,128)(2,1)S(1)}, u32[]{:S(2)}, u32[]{:S(2)}) collective-permute-start(bf16[1024,128]{1,0:T(8,128)(2,1)S(1)} %collective-permute-done.1.refs_2_), channel_id=1, source_target_pairs={{0,2},{1,3},{2,0},{3,1},{4,6},{5,7},{6,4},{7,5},{8,10},{9,11},{10,... | collective-permute-start | bytes 786440 | tf_op jit(solution)/shard_map/ppermute | solution.py:226
  19.9 7.1 %collective-permute-done.10.refs_1_ = bf16[1024,128]{1,0:T(8,128)(2,1)S(1)} collective-permute-done((bf16[1024,128]{1,0:T(8,128)(2,1)S(1)}, bf16[1024,128]{1,0:T(8,128)(2,1)S(1)}, u32[]{:S(2)}, u32[]{:S(2)}) %collective-permute-start.10) | collective-permute-done | bytes 262176 | tf_op jit(solution)/shard_map/ppermute | solution.py:226
  27.0 1.2 collective-permute-done.3.refs_4_
  28.8 1.1 collective-permute-done.2.refs_3_
  31.4 2.4 %shard_map.94 = bf16[16,272,128]{2,1,0:T(8,128)(2,1)} custom-call(s32[32]{0:T(128)S(1)} %get-tuple-element.105.slot_ref, s32[32]{0:T(128)S(1)} %get-tuple-element.108.source_ref, s32[32]{0:T(128)S(1)} %get-tuple-element.109.local_ref, bf16[32,128,128]{2,1,0:T(8,128)(2,1)S(1)} %copy-done, bf16[1024,128]{1,0:T(8,128)(2,1)S(1)} %get-tuple-element.95.refs_0_, ...), custom_call_target="tpu_custom_call" | custom-call | flops 134217728 | bytes 4194304 | tf_op jit(solution)/shard_map/pallas_call | solution.py:267
  33.8 8.7 %all-to-all-start = ((bf16[16,272,128]{2,1,0:T(8,128)(2,1)}), bf16[16,272,128]{2,1,0:T(8,128)(2,1)S(1)}, u32[]{:S(2)}, u32[]{:S(2)}) async-start(bf16[16,272,128]{2,1,0:T(8,128)(2,1)} %shard_map.94), calls=%async_computation | async-start | bytes 2228224 | tf_op jit(solution)/shard_map/all_to_all | solution.py:288
  42.6 1.5 collective-permute-start.12
  44.1 8.1 %collective-permute-done.12.refs_2_ = bf16[1024,128]{1,0:T(8,128)(2,1)S(1)} collective-permute-done((bf16[1024,128]{1,0:T(8,128)(2,1)S(1)}, bf16[1024,128]{1,0:T(8,128)(2,1)S(1)}, u32[]{:S(2)}, u32[]{:S(2)}) %collective-permute-start.12) | collective-permute-done | bytes 262176 | tf_op jit(solution)/shard_map/ppermute | solution.py:226
  52.2 0.8 collective-permute-start.14
  53.0 2.4 %collective-permute-start.15 = (bf16[2048,128]{1,0:T(8,128)(2,1)S(1)}, bf16[2048,128]{1,0:T(8,128)(2,1)S(1)}, u32[]{:S(2)}, u32[]{:S(2)}) collective-permute-start(bf16[2048,128]{1,0:T(8,128)(2,1)S(1)} %pad_maximum_fusion.1), channel_id=1, source_target_pairs={{0,4},{1,5},{2,6},{3,7},{4,8},{5,9},{6,10},{7,11},{8,12},{9,13},{1... | collective-permute-start | bytes 1572872 | tf_op jit(solution)/shard_map/ppermute | solution.py:226
  55.5 1.8 collective-permute-start.13
  57.3 8.9 %collective-permute-done.14.refs_4_ = bf16[2048,128]{1,0:T(8,128)(2,1)S(1)} collective-permute-done((bf16[2048,128]{1,0:T(8,128)(2,1)S(1)}, bf16[2048,128]{1,0:T(8,128)(2,1)S(1)}, u32[]{:S(2)}, u32[]{:S(2)}) %collective-permute-start.14) | collective-permute-done | bytes 524320 | tf_op jit(solution)/shard_map/ppermute | solution.py:226
  67.3 2.3 %collective-permute-done.13.refs_3_ = bf16[1024,128]{1,0:T(8,128)(2,1)S(1)} collective-permute-done((bf16[1024,128]{1,0:T(8,128)(2,1)S(1)}, bf16[1024,128]{1,0:T(8,128)(2,1)S(1)}, u32[]{:S(2)}, u32[]{:S(2)}) %collective-permute-start.13) | collective-permute-done | bytes 262176 | tf_op jit(solution)/shard_map/ppermute | solution.py:226
  69.7 1.4 collective-permute-done.19.refs_9_
  71.1 2.4 %shard_map.96 = bf16[16,256,128]{2,1,0:T(8,128)(2,1)} custom-call(s32[32]{0:T(128)S(1)} %get-tuple-element.105.slot_ref, s32[32]{0:T(128)S(1)} %get-tuple-element.108.source_ref, s32[32]{0:T(128)S(1)} %get-tuple-element.109.local_ref, bf16[32,128,128]{2,1,0:T(8,128)(2,1)S(1)} %copy-done, bf16[1024,128]{1,0:T(8,128)(2,1)S(1)} %get-tuple-element.50.refs_0_, ...), custom_call_target="tpu_custom_call" | custom-call | flops 134217728 | bytes 4194304 | tf_op jit(solution)/shard_map/pallas_call | solution.py:267
  73.5 8.5 %all-to-all-start.1 = ((bf16[16,256,128]{2,1,0:T(8,128)(2,1)}), bf16[16,256,128]{2,1,0:T(8,128)(2,1)}, u32[]{:S(2)}, u32[]{:S(2)}) async-start(bf16[16,256,128]{2,1,0:T(8,128)(2,1)} %shard_map.96), calls=%async_computation.1 | async-start | bytes 2097152 | tf_op jit(solution)/shard_map/all_to_all | solution.py:288
  84.8 2.0 broadcast_multiply_fusion.refs_4_
  88.6 1.0 copy-done.1
  90.1 1.1 shard_map.95.refs_2_.refs_1_
  91.8 17.6 %all-to-all-done.1.refs_1_ = bf16[16,256,128]{2,1,0:T(8,128)(2,1)} async-done(((bf16[16,256,128]{2,1,0:T(8,128)(2,1)}), bf16[16,256,128]{2,1,0:T(8,128)(2,1)}, u32[]{:S(2)}, u32[]{:S(2)}) %all-to-all-start.1) | async-done | bytes 1048608 | tf_op jit(solution)/shard_map/all_to_all | solution.py:288
  109.5 4.4 %shard_map.97 = (bf16[1024,128]{1,0:T(8,128)(2,1)}, bf16[1024,256]{1,0:T(8,128)(2,1)}, bf16[16,256,128]{2,1,0:T(8,128)(2,1)}) custom-call(s32[32]{0:T(128)} %copy-done.9, bf16[16,256,128]{2,1,0:T(8,128)(2,1)} %all-to-all-done.1.refs_1_, bf16[1024,128]{1,0:T(8,128)(2,1)} %copy-done.5, bf16[256,256]{1,0:T(8,128)(2,1)} %refs_4_.1, ...), custom_call_target="tpu_custom_call" | custom-call | flops 134217728 | bytes 2621440 | tf_op jit(solution)/shard_map/pallas_call | solution.py:326
  113.9 4.4 %all-to-all-start.2 = ((bf16[16,256,128]{2,1,0:T(8,128)(2,1)}), bf16[16,256,128]{2,1,0:T(8,128)(2,1)S(1)}, u32[]{:S(2)}, u32[]{:S(2)}) async-start(bf16[16,256,128]{2,1,0:T(8,128)(2,1)} %get-tuple-element.56), calls=%async_computation.2 | async-start | bytes 2097152 | tf_op jit(solution)/shard_map/all_to_all | solution.py:288
  118.3 3.2 %shard_map.98 = (bf16[1024,256]{1,0:T(8,128)(2,1)}, bf16[16,288,128]{2,1,0:T(8,128)(2,1)}, f32[256,256]{1,0:T(8,128)}) custom-call(s32[32]{0:T(128)} %copy-done.9, bf16[1024,128]{1,0:T(8,128)(2,1)} %copy-done.5, bf16[1024,128]{1,0:T(8,128)(2,1)} %get-tuple-element.53.refs_2_, bf16[1024,256]{1,0:T(8,128)(2,1)} %get-tuple-element.54.refs_3_, ...), custom_call_target="tpu_custom_call" | custom-call | flops 268435456 | bytes 2097152 | tf_op jit(solution)/shard_map/pallas_call | solution.py:353
  121.5 0.9 constant_dynamic-slice_fusion.4
  122.6 1.3 collective-permute-done.30
  123.9 0.9 dynamic-slice_add_fusion
  124.8 2.6 %collective-permute-start.31 = (f32[64,256]{1,0:T(8,128)S(1)}, f32[64,256]{1,0:T(8,128)S(1)}, u32[]{:S(2)}, u32[]{:S(2)}) collective-permute-start(f32[64,256]{1,0:T(8,128)S(1)} %constant_dynamic-slice_fusion.3), channel_id=1, source_target_pairs={{0,2},{1,3},{2,0},{3,1},{4,6},{5,7},{6,4},{7,5},{8,10},{9,11},{10,... | collective-permute-start | bytes 196616 | tf_op jit(solution)/shard_map/ppermute | solution.py:226
  127.4 3.5 %collective-permute-done.31 = f32[64,256]{1,0:T(8,128)S(1)} collective-permute-done((f32[64,256]{1,0:T(8,128)S(1)}, f32[64,256]{1,0:T(8,128)S(1)}, u32[]{:S(2)}, u32[]{:S(2)}) %collective-permute-start.31) | collective-permute-done | bytes 65568 | tf_op jit(solution)/shard_map/ppermute | solution.py:226
  131.0 1.3 collective-permute-start.32
  132.4 1.2 collective-permute-start.33
  133.6 1.3 collective-permute-done.32
  134.8 2.8 %collective-permute-done.33 = f32[16,256]{1,0:T(8,128)S(1)} collective-permute-done((f32[16,256]{1,0:T(8,128)S(1)}, f32[16,256]{1,0:T(8,128)S(1)}, u32[]{:S(2)}, u32[]{:S(2)}) %collective-permute-start.33) | collective-permute-done | bytes 16416 | tf_op jit(solution)/shard_map/ppermute | solution.py:226
  137.6 0.9 collective-permute-done.34
  139.2 6.3 %all-to-all-done.2.refs_10_ = bf16[16,256,128]{2,1,0:T(8,128)(2,1)S(1)} async-done(((bf16[16,256,128]{2,1,0:T(8,128)(2,1)}), bf16[16,256,128]{2,1,0:T(8,128)(2,1)S(1)}, u32[]{:S(2)}, u32[]{:S(2)}) %all-to-all-start.2) | async-done | bytes 1048608 | tf_op jit(solution)/shard_map/all_to_all | solution.py:288
  145.6 1.0 copy-done.3
  146.5 4.4 %all-to-all-start.3 = ((bf16[16,288,128]{2,1,0:T(8,128)(2,1)}), bf16[16,288,128]{2,1,0:T(8,128)(2,1)S(1)}, u32[]{:S(2)}, u32[]{:S(2)}) async-start(bf16[16,288,128]{2,1,0:T(8,128)(2,1)} %broadcast_dynamic-update-slice_fusion), calls=%async_computation.3 | async-start | bytes 2359296 | tf_op jit(solution)/shard_map/all_to_all | solution.py:288
  151.1 2.9 %collective-permute-done.24.refs_11_ = bf16[16,256,128]{2,1,0:T(8,128)(2,1)S(1)} collective-permute-done((bf16[16,256,128]{2,1,0:T(8,128)(2,1)}, bf16[16,256,128]{2,1,0:T(8,128)(2,1)S(1)}, u32[]{:S(2)}, u32[]{:S(2)}) %collective-permute-start.24) | collective-permute-done | bytes 1048608 | tf_op jit(solution)/shard_map/ppermute | solution.py:226
  153.9 1.2 copy-done.4
  155.2 4.2 %shard_map.99 = (bf16[1024,128]{1,0:T(8,128)(2,1)S(1)}, bf16[1024,128]{1,0:T(8,128)(2,1)S(1)}, bf16[1024,128]{1,0:T(8,128)(2,1)S(1)}, bf16[1024,128]{1,0:T(8,128...) custom-call(s32[1]{0:T(128)} %bitcast.1.refs_0_, s32[32]{0:T(128)S(1)} %get-tuple-element.84.refs_1_, ...), custom_call_target="tpu_custom_call" | custom-call | flops 134217728 | bytes 4194304 | tf_op jit(solution)/shard_map/pallas_call | solution.py:375
  160.4 1.3 collective-permute-start.25
  162.4 2.7 %collective-permute-start.28 = (bf16[1024,128]{1,0:T(8,128)(2,1)S(1)}, bf16[1024,128]{1,0:T(8,128)(2,1)S(1)}, u32[]{:S(2)}, u32[]{:S(2)}) collective-permute-start(bf16[1024,128]{1,0:T(8,128)(2,1)S(1)} %get-tuple-element.62), channel_id=1, source_target_pairs={{0,2},{1,3},{2,0},{3,1},{4,6},{5,7},{6,4},{7,5},{8,10},{9,11},{10,... | collective-permute-start | bytes 786440 | tf_op jit(solution)/shard_map/ppermute | solution.py:226
  165.1 12.6 %collective-permute-done.28 = bf16[1024,128]{1,0:T(8,128)(2,1)S(1)} collective-permute-done((bf16[1024,128]{1,0:T(8,128)(2,1)S(1)}, bf16[1024,128]{1,0:T(8,128)(2,1)S(1)}, u32[]{:S(2)}, u32[]{:S(2)}) %collective-permute-start.28) | collective-permute-done | bytes 262176 | tf_op jit(solution)/shard_map/ppermute | solution.py:226
  177.7 0.8 add_convert_fusion.5
  178.5 1.0 add_convert_fusion.6
  179.5 1.5 all-to-all-done.3.refs_10_
  181.1 1.1 collective-permute-start.29
  182.2 2.4 %collective-permute-start.27 = (bf16[1024,128]{1,0:T(8,128)(2,1)}, bf16[1024,128]{1,0:T(8,128)(2,1)S(1)}, u32[]{:S(2)}, u32[]{:S(2)}) collective-permute-start(bf16[1024,128]{1,0:T(8,128)(2,1)} %get-tuple-element.92), channel_id=1, source_target_pairs={{0,2},{1,3},{2,0},{3,1},{4,6},{5,7},{6,4},{7,5},{8,10},{9,11},{10,... | collective-permute-start | bytes 786440 | tf_op jit(solution)/shard_map/ppermute | solution.py:226
  184.6 4.7 %shard_map.100 = (bf16[1024,128]{1,0:T(8,128)(2,1)S(1)}, bf16[1024,128]{1,0:T(8,128)(2,1)S(1)}, bf16[1024,128]{1,0:T(8,128)(2,1)S(1)}, bf16[1024,128]{1,0:T(8,12...) custom-call(s32[1]{0:T(128)} %bitcast.1.refs_0_, s32[32]{0:T(128)S(1)} %get-tuple-element.84.refs_1_, ...), custom_call_target="tpu_custom_call" | custom-call | flops 134217728 | bytes 4194304 | tf_op jit(solution)/shard_map/pallas_call | solution.py:375
  190.8 0.8 collective-permute-done.29
  192.3 2.1 collective-permute-start.36
  194.4 2.4 %collective-permute-start.39 = (bf16[1024,128]{1,0:T(8,128)(2,1)}, bf16[1024,128]{1,0:T(8,128)(2,1)S(1)}, u32[]{:S(2)}, u32[]{:S(2)}) collective-permute-start(bf16[1024,128]{1,0:T(8,128)(2,1)} %get-tuple-element.78), channel_id=1, source_target_pairs={{0,2},{1,3},{2,0},{3,1},{4,6},{5,7},{6,4},{7,5},{8,10},{9,11},{10,... | collective-permute-start | bytes 786440 | tf_op jit(solution)/shard_map/ppermute | solution.py:226
  197.6 6.6 %all-to-all-start.4 = ((f32[16,32,128]{2,1,0:T(8,128)}), f32[16,32,128]{2,1,0:T(8,128)S(1)}, u32[]{:S(2)}, u32[]{:S(2)}) async-start(f32[16,32,128]{2,1,0:T(8,128)} %broadcast_in_dim.7), calls=%async_computation.4 | async-start | bytes 524288 | tf_op jit(solution)/shard_map/all_to_all | solution.py:438
  204.2 1.0 add_convert_fusion.1
  205.3 1.5 collective-permute-start.40
  206.8 9.7 %collective-permute-done.37 = bf16[2048,128]{1,0:T(8,128)(2,1)S(1)} collective-permute-done((bf16[2048,128]{1,0:T(8,128)(2,1)}, bf16[2048,128]{1,0:T(8,128)(2,1)S(1)}, u32[]{:S(2)}, u32[]{:S(2)}) %collective-permute-start.37) | collective-permute-done | bytes 524320 | tf_op jit(solution)/shard_map/ppermute | solution.py:226
  216.6 1.8 all-to-all-done.4
  219.3 5.2 %collective-permute-done.38 = bf16[1024,128]{1,0:T(8,128)(2,1)S(1)} collective-permute-done((bf16[1024,128]{1,0:T(8,128)(2,1)S(1)}, bf16[1024,128]{1,0:T(8,128)(2,1)S(1)}, u32[]{:S(2)}, u32[]{:S(2)}) %collective-permute-start.38) | collective-permute-done | bytes 262176 | tf_op jit(solution)/shard_map/ppermute | solution.py:226
  224.9 1.1 fusion
  (127 shorter events, 18.7 us)
Async XLA Ops:
  0.6 30.7 %copy-start = (bf16[32,128,128]{2,1,0:T(8,128)(2,1)S(1)}, bf16[32,128,128]{2,1,0:T(8,128)(2,1)}, u32[]{:S(2)}) copy-start(bf16[32,128,128]{2,1,0:T(8,128)(2,1)} %tiles_ref.3) | copy-start | bytes 3145732
  1.8 9.6 %collective-permute-start = (bf16[1024,128]{1,0:T(8,128)(2,1)S(1)}, bf16[1024,128]{1,0:T(8,128)(2,1)S(1)}, u32[]{:S(2)}, u32[]{:S(2)}) collective-permute-start(bf16[1024,128]{1,0:T(8,128)(2,1)S(1)} %get-tuple-element.95.refs_0_), channel_id=1, source_target_pairs={{0,2},{1,3},{2,0},{3,1},{4,6},{5,7},{6,4},{7,5},{8,10},{9,11},{10,... | collective-permute-start | bytes 786440 | tf_op jit(solution)/shard_map/ppermute | solution.py:226
  5.1 9.3 %collective-permute-start.1 = (bf16[1024,128]{1,0:T(8,128)(2,1)S(1)}, bf16[1024,128]{1,0:T(8,128)(2,1)S(1)}, u32[]{:S(2)}, u32[]{:S(2)}) collective-permute-start(bf16[1024,128]{1,0:T(8,128)(2,1)S(1)} %get-tuple-element.95.refs_0_), channel_id=1, source_target_pairs={{0,8},{1,9},{2,10},{3,11},{4,12},{5,13},{6,14},{7,15},{8,0},{9,1},... | collective-permute-start | bytes 786440 | tf_op jit(solution)/shard_map/ppermute | solution.py:226
  14.3 12.7 %collective-permute-start.4 = (bf16[2048,128]{1,0:T(8,128)(2,1)S(1)}, bf16[2048,128]{1,0:T(8,128)(2,1)S(1)}, u32[]{:S(2)}, u32[]{:S(2)}) collective-permute-start(bf16[2048,128]{1,0:T(8,128)(2,1)S(1)} %pad_maximum_fusion), channel_id=1, source_target_pairs={{0,4},{1,5},{2,6},{3,7},{4,8},{5,9},{6,10},{7,11},{8,12},{9,13},{1... | collective-permute-start | bytes 1572872 | tf_op jit(solution)/shard_map/ppermute | solution.py:226
  14.8 13.4 %collective-permute-start.3 = (bf16[2048,128]{1,0:T(8,128)(2,1)S(1)}, bf16[2048,128]{1,0:T(8,128)(2,1)S(1)}, u32[]{:S(2)}, u32[]{:S(2)}) collective-permute-start(bf16[2048,128]{1,0:T(8,128)(2,1)S(1)} %pad_maximum_fusion), channel_id=1, source_target_pairs={{0,12},{1,13},{2,14},{3,15},{4,0},{5,1},{6,2},{7,3},{8,4},{9,5},{1... | collective-permute-start | bytes 1572872 | tf_op jit(solution)/shard_map/ppermute | solution.py:226
  16.4 10.6 %collective-permute-start.10 = (bf16[1024,128]{1,0:T(8,128)(2,1)S(1)}, bf16[1024,128]{1,0:T(8,128)(2,1)S(1)}, u32[]{:S(2)}, u32[]{:S(2)}) collective-permute-start(bf16[1024,128]{1,0:T(8,128)(2,1)S(1)} %get-tuple-element.50.refs_0_), channel_id=1, source_target_pairs={{0,2},{1,3},{2,0},{3,1},{4,6},{5,7},{6,4},{7,5},{8,10},{9,11},{10,... | collective-permute-start | bytes 786440 | tf_op jit(solution)/shard_map/ppermute | solution.py:226
  16.8 12.0 %collective-permute-start.5 = (bf16[1024,128]{1,0:T(8,128)(2,1)S(1)}, bf16[1024,128]{1,0:T(8,128)(2,1)S(1)}, u32[]{:S(2)}, u32[]{:S(2)}) collective-permute-start(bf16[1024,128]{1,0:T(8,128)(2,1)S(1)} %get-tuple-element.95.refs_0_), channel_id=1, source_target_pairs={{0,1},{1,0},{2,3},{3,2},{4,5},{5,4},{6,7},{7,6},{8,9},{9,8},{10,11... | collective-permute-start | bytes 786440 | tf_op jit(solution)/shard_map/ppermute | solution.py:226
  16.8 13.0 %collective-permute-start.2 = (bf16[1024,128]{1,0:T(8,128)(2,1)S(1)}, bf16[1024,128]{1,0:T(8,128)(2,1)S(1)}, u32[]{:S(2)}, u32[]{:S(2)}) collective-permute-start(bf16[1024,128]{1,0:T(8,128)(2,1)S(1)} %collective-permute-done.1.refs_2_), channel_id=1, source_target_pairs={{0,2},{1,3},{2,0},{3,1},{4,6},{5,7},{6,4},{7,5},{8,10},{9,11},{10,... | collective-permute-start | bytes 786440 | tf_op jit(solution)/shard_map/ppermute | solution.py:226
  27.0 4.3 %collective-permute-start.11 = (bf16[2048,128]{1,0:T(8,128)(2,1)S(1)}, bf16[2048,128]{1,0:T(8,128)(2,1)S(1)}, u32[]{:S(2)}, u32[]{:S(2)}) collective-permute-start(bf16[2048,128]{1,0:T(8,128)(2,1)S(1)} %collective-permute-done.4.refs_5_), channel_id=1, source_target_pairs={{0,1},{1,0},{2,3},{3,2},{4,5},{5,4},{6,7},{7,6},{8,9},{9,8},{10,11... | collective-permute-start | bytes 1572872 | tf_op jit(solution)/shard_map/ppermute | solution.py:226
  28.2 3.1 %collective-permute-start.9 = (bf16[2048,128]{1,0:T(8,128)(2,1)S(1)}, bf16[2048,128]{1,0:T(8,128)(2,1)S(1)}, u32[]{:S(2)}, u32[]{:S(2)}) collective-permute-start(bf16[2048,128]{1,0:T(8,128)(2,1)S(1)} %collective-permute-done.3.refs_4_), channel_id=1, source_target_pairs={{0,1},{1,0},{2,3},{3,2},{4,5},{5,4},{6,7},{7,6},{8,9},{9,8},{10,11... | collective-permute-start | bytes 1572872 | tf_op jit(solution)/shard_map/ppermute | solution.py:226
  28.2 2.3 %collective-permute-start.7 = (bf16[1024,128]{1,0:T(8,128)(2,1)S(1)}, bf16[1024,128]{1,0:T(8,128)(2,1)S(1)}, u32[]{:S(2)}, u32[]{:S(2)}) collective-permute-start(bf16[1024,128]{1,0:T(8,128)(2,1)S(1)} %collective-permute-done.1.refs_2_), channel_id=1, source_target_pairs={{0,1},{1,0},{2,3},{3,2},{4,5},{5,4},{6,7},{7,6},{8,9},{9,8},{10,11... | collective-permute-start | bytes 786440 | tf_op jit(solution)/shard_map/ppermute | solution.py:226
  28.7 2.1 collective-permute-start.6
  29.8 1.5 collective-permute-start.8
  33.8 39.7 %all-to-all-start = ((bf16[16,272,128]{2,1,0:T(8,128)(2,1)}), bf16[16,272,128]{2,1,0:T(8,128)(2,1)S(1)}, u32[]{:S(2)}, u32[]{:S(2)}) async-start(bf16[16,272,128]{2,1,0:T(8,128)(2,1)} %shard_map.94), calls=%async_computation | async-start | bytes 2228224 | tf_op jit(solution)/shard_map/all_to_all | solution.py:288
  42.6 9.7 %collective-permute-start.12 = (bf16[1024,128]{1,0:T(8,128)(2,1)S(1)}, bf16[1024,128]{1,0:T(8,128)(2,1)S(1)}, u32[]{:S(2)}, u32[]{:S(2)}) collective-permute-start(bf16[1024,128]{1,0:T(8,128)(2,1)S(1)} %get-tuple-element.50.refs_0_), channel_id=1, source_target_pairs={{0,8},{1,9},{2,10},{3,11},{4,12},{5,13},{6,14},{7,15},{8,0},{9,1},... | collective-permute-start | bytes 786440 | tf_op jit(solution)/shard_map/ppermute | solution.py:226
  52.2 14.0 %collective-permute-start.14 = (bf16[2048,128]{1,0:T(8,128)(2,1)S(1)}, bf16[2048,128]{1,0:T(8,128)(2,1)S(1)}, u32[]{:S(2)}, u32[]{:S(2)}) collective-permute-start(bf16[2048,128]{1,0:T(8,128)(2,1)S(1)} %pad_maximum_fusion.1), channel_id=1, source_target_pairs={{0,12},{1,13},{2,14},{3,15},{4,0},{5,1},{6,2},{7,3},{8,4},{9,5},{1... | collective-permute-start | bytes 1572872 | tf_op jit(solution)/shard_map/ppermute | solution.py:226
  53.0 13.2 %collective-permute-start.15 = (bf16[2048,128]{1,0:T(8,128)(2,1)S(1)}, bf16[2048,128]{1,0:T(8,128)(2,1)S(1)}, u32[]{:S(2)}, u32[]{:S(2)}) collective-permute-start(bf16[2048,128]{1,0:T(8,128)(2,1)S(1)} %pad_maximum_fusion.1), channel_id=1, source_target_pairs={{0,4},{1,5},{2,6},{3,7},{4,8},{5,9},{6,10},{7,11},{8,12},{9,13},{1... | collective-permute-start | bytes 1572872 | tf_op jit(solution)/shard_map/ppermute | solution.py:226
  55.5 11.3 %collective-permute-start.16 = (bf16[1024,128]{1,0:T(8,128)(2,1)S(1)}, bf16[1024,128]{1,0:T(8,128)(2,1)S(1)}, u32[]{:S(2)}, u32[]{:S(2)}) collective-permute-start(bf16[1024,128]{1,0:T(8,128)(2,1)S(1)} %get-tuple-element.50.refs_0_), channel_id=1, source_target_pairs={{0,1},{1,0},{2,3},{3,2},{4,5},{5,4},{6,7},{7,6},{8,9},{9,8},{10,11... | collective-permute-start | bytes 786440 | tf_op jit(solution)/shard_map/ppermute | solution.py:226
  55.5 14.1 %collective-permute-start.13 = (bf16[1024,128]{1,0:T(8,128)(2,1)S(1)}, bf16[1024,128]{1,0:T(8,128)(2,1)S(1)}, u32[]{:S(2)}, u32[]{:S(2)}) collective-permute-start(bf16[1024,128]{1,0:T(8,128)(2,1)S(1)} %collective-permute-done.12.refs_2_), channel_id=1, source_target_pairs={{0,2},{1,3},{2,0},{3,1},{4,6},{5,7},{6,4},{7,5},{8,10},{9,11},{10,... | collective-permute-start | bytes 786440 | tf_op jit(solution)/shard_map/ppermute | solution.py:226
  66.2 4.9 %collective-permute-start.20 = (bf16[2048,128]{1,0:T(8,128)(2,1)S(1)}, bf16[2048,128]{1,0:T(8,128)(2,1)S(1)}, u32[]{:S(2)}, u32[]{:S(2)}) collective-permute-start(bf16[2048,128]{1,0:T(8,128)(2,1)S(1)} %collective-permute-done.14.refs_4_), channel_id=1, source_target_pairs={{0,1},{1,0},{2,3},{3,2},{4,5},{5,4},{6,7},{7,6},{8,9},{9,8},{10,11... | collective-permute-start | bytes 1572872 | tf_op jit(solution)/shard_map/ppermute | solution.py:226
  66.2 4.9 %collective-permute-start.21 = (bf16[2048,128]{1,0:T(8,128)(2,1)S(1)}, bf16[2048,128]{1,0:T(8,128)(2,1)S(1)}, u32[]{:S(2)}, u32[]{:S(2)}) collective-permute-start(bf16[2048,128]{1,0:T(8,128)(2,1)S(1)} %collective-permute-done.15.refs_5_), channel_id=1, source_target_pairs={{0,1},{1,0},{2,3},{3,2},{4,5},{5,4},{6,7},{7,6},{8,9},{9,8},{10,11... | collective-permute-start | bytes 1572872 | tf_op jit(solution)/shard_map/ppermute | solution.py:226
  66.8 2.9 %collective-permute-start.17 = (bf16[1024,128]{1,0:T(8,128)(2,1)S(1)}, bf16[1024,128]{1,0:T(8,128)(2,1)S(1)}, u32[]{:S(2)}, u32[]{:S(2)}) collective-permute-start(bf16[1024,128]{1,0:T(8,128)(2,1)S(1)} %collective-permute-done.10.refs_1_), channel_id=1, source_target_pairs={{0,1},{1,0},{2,3},{3,2},{4,5},{5,4},{6,7},{7,6},{8,9},{9,8},{10,11... | collective-permute-start | bytes 786440 | tf_op jit(solution)/shard_map/ppermute | solution.py:226
  66.8 2.9 %collective-permute-start.18 = (bf16[1024,128]{1,0:T(8,128)(2,1)S(1)}, bf16[1024,128]{1,0:T(8,128)(2,1)S(1)}, u32[]{:S(2)}, u32[]{:S(2)}) collective-permute-start(bf16[1024,128]{1,0:T(8,128)(2,1)S(1)} %collective-permute-done.12.refs_2_), channel_id=1, source_target_pairs={{0,1},{1,0},{2,3},{3,2},{4,5},{5,4},{6,7},{7,6},{8,9},{9,8},{10,11... | collective-permute-start | bytes 786440 | tf_op jit(solution)/shard_map/ppermute | solution.py:226
  69.6 1.5 collective-permute-start.19
  73.5 35.9 %all-to-all-start.1 = ((bf16[16,256,128]{2,1,0:T(8,128)(2,1)}), bf16[16,256,128]{2,1,0:T(8,128)(2,1)}, u32[]{:S(2)}, u32[]{:S(2)}) async-start(bf16[16,256,128]{2,1,0:T(8,128)(2,1)} %shard_map.96), calls=%async_computation.1 | async-start | bytes 2097152 | tf_op jit(solution)/shard_map/all_to_all | solution.py:288
  82.0 1.4 copy-start.20
  82.0 5.0 %collective-permute-start.23 = (s32[2,32]{1,0:T(2,128)S(1)}, s32[2,32]{1,0:T(2,128)S(1)}, u32[]{:S(2)}, u32[]{:S(2)}) collective-permute-start(s32[2,32]{1,0:T(2,128)S(1)} %pad_add_fusion), channel_id=1, source_target_pairs={{0,1},{1,0},{2,3},{3,2},{4,5},{5,4},{6,7},{7,6},{8,9},{9,8},{10,11... | collective-permute-start | bytes 776 | tf_op jit(solution)/shard_map/ppermute | solution.py:226
  82.8 5.8 %collective-permute-start.22 = (bf16[32,128,128]{2,1,0:T(8,128)(2,1)S(1)}, bf16[32,128,128]{2,1,0:T(8,128)(2,1)S(1)}, u32[]{:S(2)}, u32[]{:S(2)}) collective-permute-start(bf16[32,128,128]{2,1,0:T(8,128)(2,1)S(1)} %bitcast.37), channel_id=1, source_target_pairs={{0,1},{1,0},{2,3},{3,2},{4,5},{5,4},{6,7},{7,6},{8,9},{9,8},{10,11... | collective-permute-start | bytes 3145736 | tf_op jit(solution)/shard_map/ppermute | solution.py:226
  88.6 1.0 copy-start.1
  90.0 19.4 %copy-start.9 = (s32[32]{0:T(128)}, s32[32]{0:T(128)S(1)}, u32[]{:S(2)}) copy-start(s32[32]{0:T(128)S(1)} %reshape.524.refs_0_) | copy-start | bytes 388
  91.1 0.7 copy-start.5
  113.9 31.7 %all-to-all-start.2 = ((bf16[16,256,128]{2,1,0:T(8,128)(2,1)}), bf16[16,256,128]{2,1,0:T(8,128)(2,1)S(1)}, u32[]{:S(2)}, u32[]{:S(2)}) async-start(bf16[16,256,128]{2,1,0:T(8,128)(2,1)} %get-tuple-element.56), calls=%async_computation.2 | async-start | bytes 2097152 | tf_op jit(solution)/shard_map/all_to_all | solution.py:288
  122.4 1.4 collective-permute-start.30
  124.8 6.1 %collective-permute-start.31 = (f32[64,256]{1,0:T(8,128)S(1)}, f32[64,256]{1,0:T(8,128)S(1)}, u32[]{:S(2)}, u32[]{:S(2)}) collective-permute-start(f32[64,256]{1,0:T(8,128)S(1)} %constant_dynamic-slice_fusion.3), channel_id=1, source_target_pairs={{0,2},{1,3},{2,0},{3,1},{4,6},{5,7},{6,4},{7,5},{8,10},{9,11},{10,... | collective-permute-start | bytes 196616 | tf_op jit(solution)/shard_map/ppermute | solution.py:226
  131.0 3.8 %collective-permute-start.32 = (f32[16,256]{1,0:T(8,128)S(1)}, f32[16,256]{1,0:T(8,128)S(1)}, u32[]{:S(2)}, u32[]{:S(2)}) collective-permute-start(f32[16,256]{1,0:T(8,128)S(1)} %get-tuple-element.98), channel_id=1, source_target_pairs={{0,4},{1,5},{2,6},{3,7},{4,8},{5,9},{6,10},{7,11},{8,12},{9,13},{1... | collective-permute-start | bytes 49160 | tf_op jit(solution)/shard_map/ppermute | solution.py:226
  132.4 5.2 %collective-permute-start.33 = (f32[16,256]{1,0:T(8,128)S(1)}, f32[16,256]{1,0:T(8,128)S(1)}, u32[]{:S(2)}, u32[]{:S(2)}) collective-permute-start(f32[16,256]{1,0:T(8,128)S(1)} %get-tuple-element.96), channel_id=1, source_target_pairs={{0,8},{1,9},{2,10},{3,11},{4,12},{5,13},{6,14},{7,15},{8,0},{9,1},... | collective-permute-start | bytes 49160 | tf_op jit(solution)/shard_map/ppermute | solution.py:226
  133.6 4.9 %collective-permute-start.34 = (f32[16,256]{1,0:T(8,128)S(1)}, f32[16,256]{1,0:T(8,128)S(1)}, u32[]{:S(2)}, u32[]{:S(2)}) collective-permute-start(f32[16,256]{1,0:T(8,128)S(1)} %get-tuple-element.97), channel_id=1, source_target_pairs={{0,12},{1,13},{2,14},{3,15},{4,0},{5,1},{6,2},{7,3},{8,4},{9,5},{1... | collective-permute-start | bytes 49160 | tf_op jit(solution)/shard_map/ppermute | solution.py:226
  139.2 14.7 %copy-start.2 = (bf16[32,128,128]{2,1,0:T(8,128)(2,1)S(1)}, bf16[32,128,128]{2,1,0:T(8,128)(2,1)}, u32[]{:S(2)}) copy-start(bf16[32,128,128]{2,1,0:T(8,128)(2,1)} %copy-done.1) | copy-start | bytes 3145732
  145.6 1.0 copy-start.3
  146.5 34.4 %all-to-all-start.3 = ((bf16[16,288,128]{2,1,0:T(8,128)(2,1)}), bf16[16,288,128]{2,1,0:T(8,128)(2,1)S(1)}, u32[]{:S(2)}, u32[]{:S(2)}) async-start(bf16[16,288,128]{2,1,0:T(8,128)(2,1)} %broadcast_dynamic-update-slice_fusion), calls=%async_computation.3 | async-start | bytes 2359296 | tf_op jit(solution)/shard_map/all_to_all | solution.py:288
  151.0 3.0 %collective-permute-start.24 = (bf16[16,256,128]{2,1,0:T(8,128)(2,1)}, bf16[16,256,128]{2,1,0:T(8,128)(2,1)S(1)}, u32[]{:S(2)}, u32[]{:S(2)}) collective-permute-start(bf16[16,256,128]{2,1,0:T(8,128)(2,1)} %copy-done.3), channel_id=1, source_target_pairs={{0,1},{1,0},{2,3},{3,2},{4,5},{5,4},{6,7},{7,6},{8,9},{9,8},{10,11... | collective-permute-start | bytes 3145736 | tf_op jit(solution)/shard_map/ppermute | solution.py:226
  153.9 1.2 copy-start.4
  160.4 18.1 %collective-permute-start.25 = (bf16[2048,128]{1,0:T(8,128)(2,1)S(1)}, bf16[2048,128]{1,0:T(8,128)(2,1)S(1)}, u32[]{:S(2)}, u32[]{:S(2)}) collective-permute-start(bf16[2048,128]{1,0:T(8,128)(2,1)S(1)} %get-tuple-element.58), channel_id=1, source_target_pairs={{0,4},{1,5},{2,6},{3,7},{4,8},{5,9},{6,10},{7,11},{8,12},{9,13},{1... | collective-permute-start | bytes 1572872 | tf_op jit(solution)/shard_map/ppermute | solution.py:226
  161.7 16.8 %collective-permute-start.26 = (bf16[2048,128]{1,0:T(8,128)(2,1)S(1)}, bf16[2048,128]{1,0:T(8,128)(2,1)S(1)}, u32[]{:S(2)}, u32[]{:S(2)}) collective-permute-start(bf16[2048,128]{1,0:T(8,128)(2,1)S(1)} %get-tuple-element.59), channel_id=1, source_target_pairs={{0,12},{1,13},{2,14},{3,15},{4,0},{5,1},{6,2},{7,3},{8,4},{9,5},{1... | collective-permute-start | bytes 1572872 | tf_op jit(solution)/shard_map/ppermute | solution.py:226
  162.4 15.3 %collective-permute-start.28 = (bf16[1024,128]{1,0:T(8,128)(2,1)S(1)}, bf16[1024,128]{1,0:T(8,128)(2,1)S(1)}, u32[]{:S(2)}, u32[]{:S(2)}) collective-permute-start(bf16[1024,128]{1,0:T(8,128)(2,1)S(1)} %get-tuple-element.62), channel_id=1, source_target_pairs={{0,2},{1,3},{2,0},{3,1},{4,6},{5,7},{6,4},{7,5},{8,10},{9,11},{10,... | collective-permute-start | bytes 786440 | tf_op jit(solution)/shard_map/ppermute | solution.py:226
  180.9 3.7 %copy-start.11 = (s32[32]{0:T(128)S(1)}, s32[32]{0:T(128)}, u32[]{:S(2)}) copy-start(s32[32]{0:T(128)} %copy-done.10) | copy-start | bytes 388
  180.9 3.7 %copy-start.13 = (s32[32]{0:T(128)S(1)}, s32[32]{0:T(128)}, u32[]{:S(2)}) copy-start(s32[32]{0:T(128)} %copy-done.12) | copy-start | bytes 388
  181.0 3.6 %collective-permute-start.35 = (bf16[16,256,128]{2,1,0:T(8,128)(2,1)S(1)}, bf16[16,256,128]{2,1,0:T(8,128)(2,1)S(1)}, u32[]{:S(2)}, u32[]{:S(2)}) collective-permute-start(bf16[16,256,128]{2,1,0:T(8,128)(2,1)S(1)} %slice.93), channel_id=1, source_target_pairs={{0,1},{1,0},{2,3},{3,2},{4,5},{5,4},{6,7},{7,6},{8,9},{9,8},{10,11... | collective-permute-start | bytes 3145736 | tf_op jit(solution)/shard_map/ppermute | solution.py:226
  181.1 10.4 %collective-permute-start.29 = (bf16[1024,128]{1,0:T(8,128)(2,1)}, bf16[1024,128]{1,0:T(8,128)(2,1)S(1)}, u32[]{:S(2)}, u32[]{:S(2)}) collective-permute-start(bf16[1024,128]{1,0:T(8,128)(2,1)} %add_convert_fusion.5), channel_id=1, source_target_pairs={{0,8},{1,9},{2,10},{3,11},{4,12},{5,13},{6,14},{7,15},{8,0},{9,1},... | collective-permute-start | bytes 786440 | tf_op jit(solution)/shard_map/ppermute | solution.py:226
  182.2 10.1 %collective-permute-start.27 = (bf16[1024,128]{1,0:T(8,128)(2,1)}, bf16[1024,128]{1,0:T(8,128)(2,1)S(1)}, u32[]{:S(2)}, u32[]{:S(2)}) collective-permute-start(bf16[1024,128]{1,0:T(8,128)(2,1)} %get-tuple-element.92), channel_id=1, source_target_pairs={{0,2},{1,3},{2,0},{3,1},{4,6},{5,7},{6,4},{7,5},{8,10},{9,11},{10,... | collective-permute-start | bytes 786440 | tf_op jit(solution)/shard_map/ppermute | solution.py:226
  189.3 0.7 copy-start.6
  191.6 5.3 %copy-start.16 = (bf16[1024,128]{1,0:T(8,128)(2,1)}, bf16[1024,128]{1,0:T(8,128)(2,1)S(1)}, u32[]{:S(2)}) copy-start(bf16[1024,128]{1,0:T(8,128)(2,1)S(1)} %collective-permute-done.29) | copy-start | bytes 786436
  191.6 24.9 %copy-start.8 = (bf16[1024,128]{1,0:T(8,128)(2,1)S(1)}, bf16[1024,128]{1,0:T(8,128)(2,1)}, u32[]{:S(2)}) copy-start(bf16[1024,128]{1,0:T(8,128)(2,1)} %copy-done.7) | copy-start | bytes 786436
  192.3 4.5 %copy-start.18 = (bf16[1024,128]{1,0:T(8,128)(2,1)}, bf16[1024,128]{1,0:T(8,128)(2,1)S(1)}, u32[]{:S(2)}) copy-start(bf16[1024,128]{1,0:T(8,128)(2,1)S(1)} %collective-permute-done.27) | copy-start | bytes 786436
  192.3 14.4 %collective-permute-start.36 = (bf16[2048,128]{1,0:T(8,128)(2,1)}, bf16[2048,128]{1,0:T(8,128)(2,1)S(1)}, u32[]{:S(2)}, u32[]{:S(2)}) collective-permute-start(bf16[2048,128]{1,0:T(8,128)(2,1)} %get-tuple-element.74), channel_id=1, source_target_pairs={{0,4},{1,5},{2,6},{3,7},{4,8},{5,9},{6,10},{7,11},{8,12},{9,13},{1... | collective-permute-start | bytes 1572872 | tf_op jit(solution)/shard_map/ppermute | solution.py:226
  194.4 22.0 %collective-permute-start.37 = (bf16[2048,128]{1,0:T(8,128)(2,1)}, bf16[2048,128]{1,0:T(8,128)(2,1)S(1)}, u32[]{:S(2)}, u32[]{:S(2)}) collective-permute-start(bf16[2048,128]{1,0:T(8,128)(2,1)} %get-tuple-element.75), channel_id=1, source_target_pairs={{0,12},{1,13},{2,14},{3,15},{4,0},{5,1},{6,2},{7,3},{8,4},{9,5},{1... | collective-permute-start | bytes 1572872 | tf_op jit(solution)/shard_map/ppermute | solution.py:226
  194.4 9.8 %collective-permute-start.39 = (bf16[1024,128]{1,0:T(8,128)(2,1)}, bf16[1024,128]{1,0:T(8,128)(2,1)S(1)}, u32[]{:S(2)}, u32[]{:S(2)}) collective-permute-start(bf16[1024,128]{1,0:T(8,128)(2,1)} %get-tuple-element.78), channel_id=1, source_target_pairs={{0,2},{1,3},{2,0},{3,1},{4,6},{5,7},{6,4},{7,5},{8,10},{9,11},{10,... | collective-permute-start | bytes 786440 | tf_op jit(solution)/shard_map/ppermute | solution.py:226
  197.6 20.8 %all-to-all-start.4 = ((f32[16,32,128]{2,1,0:T(8,128)}), f32[16,32,128]{2,1,0:T(8,128)S(1)}, u32[]{:S(2)}, u32[]{:S(2)}) async-start(f32[16,32,128]{2,1,0:T(8,128)} %broadcast_in_dim.7), calls=%async_computation.4 | async-start | bytes 524288 | tf_op jit(solution)/shard_map/all_to_all | solution.py:438
  205.3 19.3 %copy-start.14 = (bf16[256,256]{1,0:T(8,128)(2,1)S(1)}, bf16[256,256]{1,0:T(8,128)(2,1)}, u32[]{:S(2)}) copy-start(bf16[256,256]{1,0:T(8,128)(2,1)} %refs_4_.1) | copy-start | bytes 393220
  205.3 14.1 %collective-permute-start.40 = (bf16[1024,128]{1,0:T(8,128)(2,1)S(1)}, bf16[1024,128]{1,0:T(8,128)(2,1)S(1)}, u32[]{:S(2)}, u32[]{:S(2)}) collective-permute-start(bf16[1024,128]{1,0:T(8,128)(2,1)S(1)} %add_convert_fusion.1), channel_id=1, source_target_pairs={{0,8},{1,9},{2,10},{3,11},{4,12},{5,13},{6,14},{7,15},{8,0},{9,1},... | collective-permute-start | bytes 786440 | tf_op jit(solution)/shard_map/ppermute | solution.py:226
  216.5 8.0 %collective-permute-start.38 = (bf16[1024,128]{1,0:T(8,128)(2,1)S(1)}, bf16[1024,128]{1,0:T(8,128)(2,1)S(1)}, u32[]{:S(2)}, u32[]{:S(2)}) collective-permute-start(bf16[1024,128]{1,0:T(8,128)(2,1)S(1)} %add_convert_fusion.2), channel_id=1, source_target_pairs={{0,2},{1,3},{2,0},{3,1},{4,6},{5,7},{6,4},{7,5},{8,10},{9,11},{10,... | collective-permute-start | bytes 786440 | tf_op jit(solution)/shard_map/ppermute | solution.py:226
  219.3 5.5 %copy-start.15 = (bf16[1024,128]{1,0:T(8,128)(2,1)S(1)}, bf16[1024,128]{1,0:T(8,128)(2,1)}, u32[]{:S(2)}) copy-start(bf16[1024,128]{1,0:T(8,128)(2,1)} %get-tuple-element.93) | copy-start | bytes 786436
  219.3 5.5 %copy-start.17 = (bf16[1024,128]{1,0:T(8,128)(2,1)S(1)}, bf16[1024,128]{1,0:T(8,128)(2,1)}, u32[]{:S(2)}) copy-start(bf16[1024,128]{1,0:T(8,128)(2,1)} %copy-done.16) | copy-start | bytes 786436
  219.3 5.5 %copy-start.19 = (bf16[1024,128]{1,0:T(8,128)(2,1)S(1)}, bf16[1024,128]{1,0:T(8,128)(2,1)}, u32[]{:S(2)}) copy-start(bf16[1024,128]{1,0:T(8,128)(2,1)} %copy-done.18) | copy-start | bytes 786436
  (3 other events, 1.7 us)
where the time goes:
time: 227 us; the launch traced here: 226 us
  waiting for transfers between devices  107 us (47%)
  starting transfers between devices  71.5 us (31%)
  Pallas kernels  22.4 us (10%)
  local copies, waits for them, and re-layouts  11.6 us (5%)
  other arithmetic  11.2 us (5%)
    ppermute x41, waiting for transfers between devices, move(): return lax.ppermute(value, 'blk', blk_pairs(blk_count, dx, dy, dc))  79.5 us
    ppermute x41, starting transfers between devices, move(): return lax.ppermute(value, 'blk', blk_pairs(blk_count, dx, dy, dc))  38.8 us
    all_to_all x4, starting transfers between devices, exchange(): return lax.all_to_all(value, 'rows', 0, 0, tiled=True)  26 us
    all_to_all x4, waiting for transfers between devices, exchange(): return lax.all_to_all(value, 'rows', 0, 0, tiled=True)  25.4 us
    pallas_call x2, Pallas kernels, backward(): pl.pallas_call(lambda *refs: backward_kernel(block, *refs), out_shape=[ja...  8.88 us
    unnamed x44, local copies, waits for them, and re-layouts  7.75 us
    all_to_all x1, starting transfers between devices, body(): lax.all_to_all(jnp.broadcast_to(piece[None], (blk_count, *piece.shape)),...  6.63 us
    pallas_call x2, Pallas kernels, forward(): pl.pallas_call(forward_kernel, out_shape=jax.ShapeDtypeStruct((row_count,...  4.82 us
  transfers between devices with their start and end apart: 46, of which 27 were waited for; matrix products, arithmetic and copies ran while one was open for 7% of the time, Pallas kernels for 7%

commit v1 on v0

--- a/solution.py
+++ b/solution.py
@@ -398,7 +398,7 @@
     def first_sums(parts):
         own, across, twice, across_twice, plus, minus = parts
         from_minus, from_plus = move(plus, 1, 0, 0), move(minus, -1, 0, 0)
-        twice = wide_sum(twice, move(across_twice, 0, 1, 0))
+        twice = after(wide_sum(twice, move(across_twice, 0, 1, 0)), from_minus, from_plus)
         own = wide_sum(own, from_minus[:own_rows], from_plus[:own_rows])
         across = wide_sum(across, from_minus[own_rows:], from_plus[own_rows:])
         return [own, across, twice]

time: 227 us -> 224 us (0.987)
  waiting for transfers between devices: 107 us -> 103 us
  transfers between devices with their start and end apart: 46 -> 46, of which waited for: 27 -> 28; matrix products, arithmetic and copies ran while one was open for 7% -> 7% of each run, Pallas kernels for 7% -> 7%
where the time goes in v1:
time: 224 us; the launch traced here: 223 us
  waiting for transfers between devices  103 us (46%)
  starting transfers between devices  72.2 us (32%)
  Pallas kernels  22.1 us (10%)
  local copies, waits for them, and re-layouts  11.6 us (5%)
  other arithmetic  11.2 us (5%)
    ppermute x41, waiting for transfers between devices, move(): return lax.ppermute(value, 'blk', blk_pairs(blk_count, dx, dy, dc))  77.7 us
    ppermute x41, starting transfers between devices, move(): return lax.ppermute(value, 'blk', blk_pairs(blk_count, dx, dy, dc))  39.5 us
    all_to_all x4, starting transfers between devices, exchange(): return lax.all_to_all(value, 'rows', 0, 0, tiled=True)  26 us
    all_to_all x4, waiting for transfers between devices, exchange(): return lax.all_to_all(value, 'rows', 0, 0, tiled=True)  25.4 us
    pallas_call x2, Pallas kernels, backward(): pl.pallas_call(lambda *refs: backward_kernel(block, *refs), out_shape=[ja...  8.51 us
    unnamed x44, local copies, waits for them, and re-layouts  7.75 us
    all_to_all x1, starting transfers between devices, body(): lax.all_to_all(jnp.broadcast_to(piece[None], (blk_count, *piece.shape)),...  6.63 us
    pallas_call x2, Pallas kernels, forward(): pl.pallas_call(forward_kernel, out_shape=jax.ShapeDtypeStruct((row_count,...  4.82 us
  transfers between devices with their start and end apart: 46, of which 28 were waited for; matrix products, arithmetic and copies ran while one was open for 7% of the time, Pallas kernels for 7%

profile of v1, /device:TPU:6, one launch (start us, length us, event | category | flops | bytes accessed | tf_op | source)
XLA Modules:
  0.0 222.7 jit_solution(12001091103154607389)
XLA Ops:
  0.6 1.2 fusion.25
  1.8 3.3 %collective-permute-start = (bf16[1024,128]{1,0:T(8,128)(2,1)S(1)}, bf16[1024,128]{1,0:T(8,128)(2,1)S(1)}, u32[]{:S(2)}, u32[]{:S(2)}) collective-permute-start(bf16[1024,128]{1,0:T(8,128)(2,1)S(1)} %get-tuple-element.99.refs_0_), channel_id=1, source_target_pairs={{0,2},{1,3},{2,0},{3,1},{4,6},{5,7},{6,4},{7,5},{8,10},{9,11},{10,... | collective-permute-start | bytes 786440 | tf_op jit(solution)/shard_map/ppermute | solution.py:226
  5.1 1.4 collective-permute-start.1
  8.2 3.3 %collective-permute-done.refs_1_ = bf16[1024,128]{1,0:T(8,128)(2,1)S(1)} collective-permute-done((bf16[1024,128]{1,0:T(8,128)(2,1)S(1)}, bf16[1024,128]{1,0:T(8,128)(2,1)S(1)}, u32[]{:S(2)}, u32[]{:S(2)}) %collective-permute-start) | collective-permute-done | bytes 262176 | tf_op jit(solution)/shard_map/ppermute | solution.py:226
  11.5 2.9 %collective-permute-done.1.refs_2_ = bf16[1024,128]{1,0:T(8,128)(2,1)S(1)} collective-permute-done((bf16[1024,128]{1,0:T(8,128)(2,1)S(1)}, bf16[1024,128]{1,0:T(8,128)(2,1)S(1)}, u32[]{:S(2)}, u32[]{:S(2)}) %collective-permute-start.1) | collective-permute-done | bytes 262176 | tf_op jit(solution)/shard_map/ppermute | solution.py:226
  14.8 1.5 collective-permute-start.3
  16.8 3.1 %collective-permute-start.2 = (bf16[1024,128]{1,0:T(8,128)(2,1)S(1)}, bf16[1024,128]{1,0:T(8,128)(2,1)S(1)}, u32[]{:S(2)}, u32[]{:S(2)}) collective-permute-start(bf16[1024,128]{1,0:T(8,128)(2,1)S(1)} %collective-permute-done.1.refs_2_), channel_id=1, source_target_pairs={{0,2},{1,3},{2,0},{3,1},{4,6},{5,7},{6,4},{7,5},{8,10},{9,11},{10,... | collective-permute-start | bytes 786440 | tf_op jit(solution)/shard_map/ppermute | solution.py:226
  19.9 7.1 %collective-permute-done.10.refs_1_ = bf16[1024,128]{1,0:T(8,128)(2,1)S(1)} collective-permute-done((bf16[1024,128]{1,0:T(8,128)(2,1)S(1)}, bf16[1024,128]{1,0:T(8,128)(2,1)S(1)}, u32[]{:S(2)}, u32[]{:S(2)}) %collective-permute-start.10) | collective-permute-done | bytes 262176 | tf_op jit(solution)/shard_map/ppermute | solution.py:226
  27.0 1.2 collective-permute-done.3.refs_4_
  28.8 1.1 collective-permute-done.2.refs_3_
  31.4 2.4 %shard_map.94 = bf16[16,272,128]{2,1,0:T(8,128)(2,1)} custom-call(s32[32]{0:T(128)S(1)} %get-tuple-element.109.slot_ref, s32[32]{0:T(128)S(1)} %get-tuple-element.112.source_ref, s32[32]{0:T(128)S(1)} %get-tuple-element.113.local_ref, bf16[32,128,128]{2,1,0:T(8,128)(2,1)S(1)} %copy-done, bf16[1024,128]{1,0:T(8,128)(2,1)S(1)} %get-tuple-element.99.refs_0_, ...), custom_call_target="tpu_custom_call" | custom-call | flops 134217728 | bytes 4194304 | tf_op jit(solution)/shard_map/pallas_call | solution.py:267
  33.8 8.7 %all-to-all-start = ((bf16[16,272,128]{2,1,0:T(8,128)(2,1)}), bf16[16,272,128]{2,1,0:T(8,128)(2,1)S(1)}, u32[]{:S(2)}, u32[]{:S(2)}) async-start(bf16[16,272,128]{2,1,0:T(8,128)(2,1)} %shard_map.94), calls=%async_computation | async-start | bytes 2228224 | tf_op jit(solution)/shard_map/all_to_all | solution.py:288
  42.6 1.5 collective-permute-start.12
  44.1 8.1 %collective-permute-done.12.refs_2_ = bf16[1024,128]{1,0:T(8,128)(2,1)S(1)} collective-permute-done((bf16[1024,128]{1,0:T(8,128)(2,1)S(1)}, bf16[1024,128]{1,0:T(8,128)(2,1)S(1)}, u32[]{:S(2)}, u32[]{:S(2)}) %collective-permute-start.12) | collective-permute-done | bytes 262176 | tf_op jit(solution)/shard_map/ppermute | solution.py:226
  52.2 0.8 collective-permute-start.14
  53.0 2.4 %collective-permute-start.15 = (bf16[2048,128]{1,0:T(8,128)(2,1)S(1)}, bf16[2048,128]{1,0:T(8,128)(2,1)S(1)}, u32[]{:S(2)}, u32[]{:S(2)}) collective-permute-start(bf16[2048,128]{1,0:T(8,128)(2,1)S(1)} %pad_maximum_fusion.1), channel_id=1, source_target_pairs={{0,4},{1,5},{2,6},{3,7},{4,8},{5,9},{6,10},{7,11},{8,12},{9,13},{1... | collective-permute-start | bytes 1572872 | tf_op jit(solution)/shard_map/ppermute | solution.py:226
  55.5 1.8 collective-permute-start.13
  57.3 8.9 %collective-permute-done.14.refs_4_ = bf16[2048,128]{1,0:T(8,128)(2,1)S(1)} collective-permute-done((bf16[2048,128]{1,0:T(8,128)(2,1)S(1)}, bf16[2048,128]{1,0:T(8,128)(2,1)S(1)}, u32[]{:S(2)}, u32[]{:S(2)}) %collective-permute-start.14) | collective-permute-done | bytes 524320 | tf_op jit(solution)/shard_map/ppermute | solution.py:226
  67.3 2.3 %collective-permute-done.13.refs_3_ = bf16[1024,128]{1,0:T(8,128)(2,1)S(1)} collective-permute-done((bf16[1024,128]{1,0:T(8,128)(2,1)S(1)}, bf16[1024,128]{1,0:T(8,128)(2,1)S(1)}, u32[]{:S(2)}, u32[]{:S(2)}) %collective-permute-start.13) | collective-permute-done | bytes 262176 | tf_op jit(solution)/shard_map/ppermute | solution.py:226
  69.7 1.4 collective-permute-done.19.refs_9_
  71.1 2.4 %shard_map.96 = bf16[16,256,128]{2,1,0:T(8,128)(2,1)} custom-call(s32[32]{0:T(128)S(1)} %get-tuple-element.109.slot_ref, s32[32]{0:T(128)S(1)} %get-tuple-element.112.source_ref, s32[32]{0:T(128)S(1)} %get-tuple-element.113.local_ref, bf16[32,128,128]{2,1,0:T(8,128)(2,1)S(1)} %copy-done, bf16[1024,128]{1,0:T(8,128)(2,1)S(1)} %get-tuple-element.52.refs_0_, ...), custom_call_target="tpu_custom_call" | custom-call | flops 134217728 | bytes 4194304 | tf_op jit(solution)/shard_map/pallas_call | solution.py:267
  73.5 8.5 %all-to-all-start.1 = ((bf16[16,256,128]{2,1,0:T(8,128)(2,1)}), bf16[16,256,128]{2,1,0:T(8,128)(2,1)}, u32[]{:S(2)}, u32[]{:S(2)}) async-start(bf16[16,256,128]{2,1,0:T(8,128)(2,1)} %shard_map.96), calls=%async_computation.1 | async-start | bytes 2097152 | tf_op jit(solution)/shard_map/all_to_all | solution.py:288
  84.8 2.0 broadcast_multiply_fusion.refs_4_
  88.6 1.0 copy-done.1
  90.1 1.1 shard_map.95.refs_2_.refs_1_
  91.8 17.6 %all-to-all-done.1.refs_1_ = bf16[16,256,128]{2,1,0:T(8,128)(2,1)} async-done(((bf16[16,256,128]{2,1,0:T(8,128)(2,1)}), bf16[16,256,128]{2,1,0:T(8,128)(2,1)}, u32[]{:S(2)}, u32[]{:S(2)}) %all-to-all-start.1) | async-done | bytes 1048608 | tf_op jit(solution)/shard_map/all_to_all | solution.py:288
  109.5 4.4 %shard_map.97 = (bf16[1024,128]{1,0:T(8,128)(2,1)}, bf16[1024,256]{1,0:T(8,128)(2,1)}, bf16[16,256,128]{2,1,0:T(8,128)(2,1)}) custom-call(s32[32]{0:T(128)} %copy-done.9, bf16[16,256,128]{2,1,0:T(8,128)(2,1)} %all-to-all-done.1.refs_1_, bf16[1024,128]{1,0:T(8,128)(2,1)} %copy-done.5, bf16[256,256]{1,0:T(8,128)(2,1)} %refs_4_.1, ...), custom_call_target="tpu_custom_call" | custom-call | flops 134217728 | bytes 2621440 | tf_op jit(solution)/shard_map/pallas_call | solution.py:326
  113.9 4.4 %all-to-all-start.2 = ((bf16[16,256,128]{2,1,0:T(8,128)(2,1)}), bf16[16,256,128]{2,1,0:T(8,128)(2,1)S(1)}, u32[]{:S(2)}, u32[]{:S(2)}) async-start(bf16[16,256,128]{2,1,0:T(8,128)(2,1)} %get-tuple-element.58), calls=%async_computation.2 | async-start | bytes 2097152 | tf_op jit(solution)/shard_map/all_to_all | solution.py:288
  118.3 3.2 %shard_map.98 = (bf16[1024,256]{1,0:T(8,128)(2,1)}, bf16[16,288,128]{2,1,0:T(8,128)(2,1)}, f32[256,256]{1,0:T(8,128)}) custom-call(s32[32]{0:T(128)} %copy-done.9, bf16[1024,128]{1,0:T(8,128)(2,1)} %copy-done.5, bf16[1024,128]{1,0:T(8,128)(2,1)} %get-tuple-element.55.refs_2_, bf16[1024,256]{1,0:T(8,128)(2,1)} %get-tuple-element.56.refs_3_, ...), custom_call_target="tpu_custom_call" | custom-call | flops 268435456 | bytes 2097152 | tf_op jit(solution)/shard_map/pallas_call | solution.py:353
  121.5 0.9 constant_dynamic-slice_fusion.4
  122.6 1.3 collective-permute-done.30
  123.9 0.9 dynamic-slice_add_fusion
  124.8 2.6 %collective-permute-start.31 = (f32[64,256]{1,0:T(8,128)S(1)}, f32[64,256]{1,0:T(8,128)S(1)}, u32[]{:S(2)}, u32[]{:S(2)}) collective-permute-start(f32[64,256]{1,0:T(8,128)S(1)} %constant_dynamic-slice_fusion.3), channel_id=1, source_target_pairs={{0,2},{1,3},{2,0},{3,1},{4,6},{5,7},{6,4},{7,5},{8,10},{9,11},{10,... | collective-permute-start | bytes 196616 | tf_op jit(solution)/shard_map/ppermute | solution.py:226
  127.4 3.5 %collective-permute-done.31 = f32[64,256]{1,0:T(8,128)S(1)} collective-permute-done((f32[64,256]{1,0:T(8,128)S(1)}, f32[64,256]{1,0:T(8,128)S(1)}, u32[]{:S(2)}, u32[]{:S(2)}) %collective-permute-start.31) | collective-permute-done | bytes 65568 | tf_op jit(solution)/shard_map/ppermute | solution.py:226
  131.0 1.3 collective-permute-start.32
  132.4 1.2 collective-permute-start.33
  133.6 1.3 collective-permute-done.32
  134.8 2.8 %collective-permute-done.33 = f32[16,256]{1,0:T(8,128)S(1)} collective-permute-done((f32[16,256]{1,0:T(8,128)S(1)}, f32[16,256]{1,0:T(8,128)S(1)}, u32[]{:S(2)}, u32[]{:S(2)}) %collective-permute-start.33) | collective-permute-done | bytes 16416 | tf_op jit(solution)/shard_map/ppermute | solution.py:226
  137.6 0.9 collective-permute-done.34
  139.2 6.3 %all-to-all-done.2.refs_10_ = bf16[16,256,128]{2,1,0:T(8,128)(2,1)S(1)} async-done(((bf16[16,256,128]{2,1,0:T(8,128)(2,1)}), bf16[16,256,128]{2,1,0:T(8,128)(2,1)S(1)}, u32[]{:S(2)}, u32[]{:S(2)}) %all-to-all-start.2) | async-done | bytes 1048608 | tf_op jit(solution)/shard_map/all_to_all | solution.py:288
  145.6 1.0 copy-done.3
  146.5 4.4 %all-to-all-start.3 = ((bf16[16,288,128]{2,1,0:T(8,128)(2,1)}), bf16[16,288,128]{2,1,0:T(8,128)(2,1)S(1)}, u32[]{:S(2)}, u32[]{:S(2)}) async-start(bf16[16,288,128]{2,1,0:T(8,128)(2,1)} %broadcast_dynamic-update-slice_fusion), calls=%async_computation.3 | async-start | bytes 2359296 | tf_op jit(solution)/shard_map/all_to_all | solution.py:288
  151.1 2.9 %collective-permute-done.24.refs_11_ = bf16[16,256,128]{2,1,0:T(8,128)(2,1)S(1)} collective-permute-done((bf16[16,256,128]{2,1,0:T(8,128)(2,1)}, bf16[16,256,128]{2,1,0:T(8,128)(2,1)S(1)}, u32[]{:S(2)}, u32[]{:S(2)}) %collective-permute-start.24) | collective-permute-done | bytes 1048608 | tf_op jit(solution)/shard_map/ppermute | solution.py:226
  153.9 1.2 copy-done.4
  155.2 4.0 %shard_map.99 = (bf16[1024,128]{1,0:T(8,128)(2,1)S(1)}, bf16[1024,128]{1,0:T(8,128)(2,1)S(1)}, bf16[1024,128]{1,0:T(8,128)(2,1)S(1)}, bf16[1024,128]{1,0:T(8,128...) custom-call(s32[1]{0:T(128)} %bitcast.1.refs_0_, s32[32]{0:T(128)S(1)} %get-tuple-element.88.refs_1_, ...), custom_call_target="tpu_custom_call" | custom-call | flops 134217728 | bytes 4194304 | tf_op jit(solution)/shard_map/pallas_call | solution.py:375
  160.2 1.3 collective-permute-start.25
  162.2 2.5 %collective-permute-start.28 = (bf16[1024,128]{1,0:T(8,128)(2,1)S(1)}, bf16[1024,128]{1,0:T(8,128)(2,1)S(1)}, u32[]{:S(2)}, u32[]{:S(2)}) collective-permute-start(bf16[1024,128]{1,0:T(8,128)(2,1)S(1)} %get-tuple-element.64), channel_id=1, source_target_pairs={{0,2},{1,3},{2,0},{3,1},{4,6},{5,7},{6,4},{7,5},{8,10},{9,11},{10,... | collective-permute-start | bytes 786440 | tf_op jit(solution)/shard_map/ppermute | solution.py:226
  164.7 12.9 %collective-permute-done.28 = bf16[1024,128]{1,0:T(8,128)(2,1)S(1)} collective-permute-done((bf16[1024,128]{1,0:T(8,128)(2,1)S(1)}, bf16[1024,128]{1,0:T(8,128)(2,1)S(1)}, u32[]{:S(2)}, u32[]{:S(2)}) %collective-permute-start.28) | collective-permute-done | bytes 262176 | tf_op jit(solution)/shard_map/ppermute | solution.py:226
  177.7 0.8 add_convert_fusion.5
  178.5 1.0 add_convert_fusion.6
  179.5 1.4 all-to-all-done.3.refs_10_
  181.1 1.1 collective-permute-start.29
  182.2 2.4 %collective-permute-start.27 = (bf16[1024,128]{1,0:T(8,128)(2,1)}, bf16[1024,128]{1,0:T(8,128)(2,1)S(1)}, u32[]{:S(2)}, u32[]{:S(2)}) collective-permute-start(bf16[1024,128]{1,0:T(8,128)(2,1)} %get-tuple-element.96), channel_id=1, source_target_pairs={{0,2},{1,3},{2,0},{3,1},{4,6},{5,7},{6,4},{7,5},{8,10},{9,11},{10,... | collective-permute-start | bytes 786440 | tf_op jit(solution)/shard_map/ppermute | solution.py:226
  184.6 4.5 %shard_map.100 = (bf16[1024,128]{1,0:T(8,128)(2,1)S(1)}, bf16[1024,128]{1,0:T(8,128)(2,1)S(1)}, bf16[1024,128]{1,0:T(8,128)(2,1)S(1)}, bf16[1024,128]{1,0:T(8,12...) custom-call(s32[1]{0:T(128)} %bitcast.1.refs_0_, s32[32]{0:T(128)S(1)} %get-tuple-element.88.refs_1_, ...), custom_call_target="tpu_custom_call" | custom-call | flops 134217728 | bytes 4194304 | tf_op jit(solution)/shard_map/pallas_call | solution.py:375
  190.6 1.0 collective-permute-done.29
  192.3 2.1 collective-permute-start.36
  194.4 2.4 %collective-permute-start.39 = (bf16[1024,128]{1,0:T(8,128)(2,1)}, bf16[1024,128]{1,0:T(8,128)(2,1)S(1)}, u32[]{:S(2)}, u32[]{:S(2)}) collective-permute-start(bf16[1024,128]{1,0:T(8,128)(2,1)} %get-tuple-element.81), channel_id=1, source_target_pairs={{0,2},{1,3},{2,0},{3,1},{4,6},{5,7},{6,4},{7,5},{8,10},{9,11},{10,... | collective-permute-start | bytes 786440 | tf_op jit(solution)/shard_map/ppermute | solution.py:226
  197.6 6.6 %all-to-all-start.4 = ((f32[16,32,128]{2,1,0:T(8,128)}), f32[16,32,128]{2,1,0:T(8,128)S(1)}, u32[]{:S(2)}, u32[]{:S(2)}) async-start(f32[16,32,128]{2,1,0:T(8,128)} %broadcast_in_dim.7), calls=%async_computation.4 | async-start | bytes 524288 | tf_op jit(solution)/shard_map/all_to_all | solution.py:438
  204.2 1.0 add_convert_fusion.1
  205.7 5.1 %collective-permute-done.37 = bf16[2048,128]{1,0:T(8,128)(2,1)S(1)} collective-permute-done((bf16[2048,128]{1,0:T(8,128)(2,1)}, bf16[2048,128]{1,0:T(8,128)(2,1)S(1)}, u32[]{:S(2)}, u32[]{:S(2)}) %collective-permute-start.37) | collective-permute-done | bytes 524320 | tf_op jit(solution)/shard_map/ppermute | solution.py:226
  210.9 2.5 %collective-permute-start.38 = (bf16[1024,128]{1,0:T(8,128)(2,1)S(1)}, bf16[1024,128]{1,0:T(8,128)(2,1)S(1)}, u32[]{:S(2)}, u32[]{:S(2)}) collective-permute-start(bf16[1024,128]{1,0:T(8,128)(2,1)S(1)} %add_convert_fusion.2), channel_id=1, source_target_pairs={{0,2},{1,3},{2,0},{3,1},{4,6},{5,7},{6,4},{7,5},{8,10},{9,11},{10,... | collective-permute-start | bytes 786440 | tf_op jit(solution)/shard_map/ppermute | solution.py:226
  214.3 4.6 %collective-permute-done.38 = bf16[1024,128]{1,0:T(8,128)(2,1)S(1)} collective-permute-done((bf16[1024,128]{1,0:T(8,128)(2,1)S(1)}, bf16[1024,128]{1,0:T(8,128)(2,1)S(1)}, u32[]{:S(2)}, u32[]{:S(2)}) %collective-permute-start.38) | collective-permute-done | bytes 262176 | tf_op jit(solution)/shard_map/ppermute | solution.py:226
  218.9 2.4 %collective-permute-done.40 = bf16[1024,128]{1,0:T(8,128)(2,1)S(1)} collective-permute-done((bf16[1024,128]{1,0:T(8,128)(2,1)S(1)}, bf16[1024,128]{1,0:T(8,128)(2,1)S(1)}, u32[]{:S(2)}, u32[]{:S(2)}) %collective-permute-start.40) | collective-permute-done | bytes 262176 | tf_op jit(solution)/shard_map/ppermute | solution.py:226
  221.6 1.1 fusion
  (127 shorter events, 19.0 us)
Async XLA Ops:
  0.6 30.7 %copy-start = (bf16[32,128,128]{2,1,0:T(8,128)(2,1)S(1)}, bf16[32,128,128]{2,1,0:T(8,128)(2,1)}, u32[]{:S(2)}) copy-start(bf16[32,128,128]{2,1,0:T(8,128)(2,1)} %tiles_ref.3) | copy-start | bytes 3145732
  1.8 9.6 %collective-permute-start = (bf16[1024,128]{1,0:T(8,128)(2,1)S(1)}, bf16[1024,128]{1,0:T(8,128)(2,1)S(1)}, u32[]{:S(2)}, u32[]{:S(2)}) collective-permute-start(bf16[1024,128]{1,0:T(8,128)(2,1)S(1)} %get-tuple-element.99.refs_0_), channel_id=1, source_target_pairs={{0,2},{1,3},{2,0},{3,1},{4,6},{5,7},{6,4},{7,5},{8,10},{9,11},{10,... | collective-permute-start | bytes 786440 | tf_op jit(solution)/shard_map/ppermute | solution.py:226
  5.1 9.3 %collective-permute-start.1 = (bf16[1024,128]{1,0:T(8,128)(2,1)S(1)}, bf16[1024,128]{1,0:T(8,128)(2,1)S(1)}, u32[]{:S(2)}, u32[]{:S(2)}) collective-permute-start(bf16[1024,128]{1,0:T(8,128)(2,1)S(1)} %get-tuple-element.99.refs_0_), channel_id=1, source_target_pairs={{0,8},{1,9},{2,10},{3,11},{4,12},{5,13},{6,14},{7,15},{8,0},{9,1},... | collective-permute-start | bytes 786440 | tf_op jit(solution)/shard_map/ppermute | solution.py:226
  14.3 12.7 %collective-permute-start.4 = (bf16[2048,128]{1,0:T(8,128)(2,1)S(1)}, bf16[2048,128]{1,0:T(8,128)(2,1)S(1)}, u32[]{:S(2)}, u32[]{:S(2)}) collective-permute-start(bf16[2048,128]{1,0:T(8,128)(2,1)S(1)} %pad_maximum_fusion), channel_id=1, source_target_pairs={{0,4},{1,5},{2,6},{3,7},{4,8},{5,9},{6,10},{7,11},{8,12},{9,13},{1... | collective-permute-start | bytes 1572872 | tf_op jit(solution)/shard_map/ppermute | solution.py:226
  14.8 13.4 %collective-permute-start.3 = (bf16[2048,128]{1,0:T(8,128)(2,1)S(1)}, bf16[2048,128]{1,0:T(8,128)(2,1)S(1)}, u32[]{:S(2)}, u32[]{:S(2)}) collective-permute-start(bf16[2048,128]{1,0:T(8,128)(2,1)S(1)} %pad_maximum_fusion), channel_id=1, source_target_pairs={{0,12},{1,13},{2,14},{3,15},{4,0},{5,1},{6,2},{7,3},{8,4},{9,5},{1... | collective-permute-start | bytes 1572872 | tf_op jit(solution)/shard_map/ppermute | solution.py:226
  16.4 10.6 %collective-permute-start.10 = (bf16[1024,128]{1,0:T(8,128)(2,1)S(1)}, bf16[1024,128]{1,0:T(8,128)(2,1)S(1)}, u32[]{:S(2)}, u32[]{:S(2)}) collective-permute-start(bf16[1024,128]{1,0:T(8,128)(2,1)S(1)} %get-tuple-element.52.refs_0_), channel_id=1, source_target_pairs={{0,2},{1,3},{2,0},{3,1},{4,6},{5,7},{6,4},{7,5},{8,10},{9,11},{10,... | collective-permute-start | bytes 786440 | tf_op jit(solution)/shard_map/ppermute | solution.py:226
  16.8 12.0 %collective-permute-start.5 = (bf16[1024,128]{1,0:T(8,128)(2,1)S(1)}, bf16[1024,128]{1,0:T(8,128)(2,1)S(1)}, u32[]{:S(2)}, u32[]{:S(2)}) collective-permute-start(bf16[1024,128]{1,0:T(8,128)(2,1)S(1)} %get-tuple-element.99.refs_0_), channel_id=1, source_target_pairs={{0,1},{1,0},{2,3},{3,2},{4,5},{5,4},{6,7},{7,6},{8,9},{9,8},{10,11... | collective-permute-start | bytes 786440 | tf_op jit(solution)/shard_map/ppermute | solution.py:226
  16.8 13.0 %collective-permute-start.2 = (bf16[1024,128]{1,0:T(8,128)(2,1)S(1)}, bf16[1024,128]{1,0:T(8,128)(2,1)S(1)}, u32[]{:S(2)}, u32[]{:S(2)}) collective-permute-start(bf16[1024,128]{1,0:T(8,128)(2,1)S(1)} %collective-permute-done.1.refs_2_), channel_id=1, source_target_pairs={{0,2},{1,3},{2,0},{3,1},{4,6},{5,7},{6,4},{7,5},{8,10},{9,11},{10,... | collective-permute-start | bytes 786440 | tf_op jit(solution)/shard_map/ppermute | solution.py:226
  27.0 4.3 %collective-permute-start.11 = (bf16[2048,128]{1,0:T(8,128)(2,1)S(1)}, bf16[2048,128]{1,0:T(8,128)(2,1)S(1)}, u32[]{:S(2)}, u32[]{:S(2)}) collective-permute-start(bf16[2048,128]{1,0:T(8,128)(2,1)S(1)} %collective-permute-done.4.refs_5_), channel_id=1, source_target_pairs={{0,1},{1,0},{2,3},{3,2},{4,5},{5,4},{6,7},{7,6},{8,9},{9,8},{10,11... | collective-permute-start | bytes 1572872 | tf_op jit(solution)/shard_map/ppermute | solution.py:226
  28.2 3.1 %collective-permute-start.9 = (bf16[2048,128]{1,0:T(8,128)(2,1)S(1)}, bf16[2048,128]{1,0:T(8,128)(2,1)S(1)}, u32[]{:S(2)}, u32[]{:S(2)}) collective-permute-start(bf16[2048,128]{1,0:T(8,128)(2,1)S(1)} %collective-permute-done.3.refs_4_), channel_id=1, source_target_pairs={{0,1},{1,0},{2,3},{3,2},{4,5},{5,4},{6,7},{7,6},{8,9},{9,8},{10,11... | collective-permute-start | bytes 1572872 | tf_op jit(solution)/shard_map/ppermute | solution.py:226
  28.2 2.3 %collective-permute-start.7 = (bf16[1024,128]{1,0:T(8,128)(2,1)S(1)}, bf16[1024,128]{1,0:T(8,128)(2,1)S(1)}, u32[]{:S(2)}, u32[]{:S(2)}) collective-permute-start(bf16[1024,128]{1,0:T(8,128)(2,1)S(1)} %collective-permute-done.1.refs_2_), channel_id=1, source_target_pairs={{0,1},{1,0},{2,3},{3,2},{4,5},{5,4},{6,7},{7,6},{8,9},{9,8},{10,11... | collective-permute-start | bytes 786440 | tf_op jit(solution)/shard_map/ppermute | solution.py:226
  28.7 2.1 collective-permute-start.6
  29.8 1.5 collective-permute-start.8
  33.8 39.7 %all-to-all-start = ((bf16[16,272,128]{2,1,0:T(8,128)(2,1)}), bf16[16,272,128]{2,1,0:T(8,128)(2,1)S(1)}, u32[]{:S(2)}, u32[]{:S(2)}) async-start(bf16[16,272,128]{2,1,0:T(8,128)(2,1)} %shard_map.94), calls=%async_computation | async-start | bytes 2228224 | tf_op jit(solution)/shard_map/all_to_all | solution.py:288
  42.6 9.7 %collective-permute-start.12 = (bf16[1024,128]{1,0:T(8,128)(2,1)S(1)}, bf16[1024,128]{1,0:T(8,128)(2,1)S(1)}, u32[]{:S(2)}, u32[]{:S(2)}) collective-permute-start(bf16[1024,128]{1,0:T(8,128)(2,1)S(1)} %get-tuple-element.52.refs_0_), channel_id=1, source_target_pairs={{0,8},{1,9},{2,10},{3,11},{4,12},{5,13},{6,14},{7,15},{8,0},{9,1},... | collective-permute-start | bytes 786440 | tf_op jit(solution)/shard_map/ppermute | solution.py:226
  52.2 14.0 %collective-permute-start.14 = (bf16[2048,128]{1,0:T(8,128)(2,1)S(1)}, bf16[2048,128]{1,0:T(8,128)(2,1)S(1)}, u32[]{:S(2)}, u32[]{:S(2)}) collective-permute-start(bf16[2048,128]{1,0:T(8,128)(2,1)S(1)} %pad_maximum_fusion.1), channel_id=1, source_target_pairs={{0,12},{1,13},{2,14},{3,15},{4,0},{5,1},{6,2},{7,3},{8,4},{9,5},{1... | collective-permute-start | bytes 1572872 | tf_op jit(solution)/shard_map/ppermute | solution.py:226
  53.0 13.2 %collective-permute-start.15 = (bf16[2048,128]{1,0:T(8,128)(2,1)S(1)}, bf16[2048,128]{1,0:T(8,128)(2,1)S(1)}, u32[]{:S(2)}, u32[]{:S(2)}) collective-permute-start(bf16[2048,128]{1,0:T(8,128)(2,1)S(1)} %pad_maximum_fusion.1), channel_id=1, source_target_pairs={{0,4},{1,5},{2,6},{3,7},{4,8},{5,9},{6,10},{7,11},{8,12},{9,13},{1... | collective-permute-start | bytes 1572872 | tf_op jit(solution)/shard_map/ppermute | solution.py:226
  55.5 11.3 %collective-permute-start.16 = (bf16[1024,128]{1,0:T(8,128)(2,1)S(1)}, bf16[1024,128]{1,0:T(8,128)(2,1)S(1)}, u32[]{:S(2)}, u32[]{:S(2)}) collective-permute-start(bf16[1024,128]{1,0:T(8,128)(2,1)S(1)} %get-tuple-element.52.refs_0_), channel_id=1, source_target_pairs={{0,1},{1,0},{2,3},{3,2},{4,5},{5,4},{6,7},{7,6},{8,9},{9,8},{10,11... | collective-permute-start | bytes 786440 | tf_op jit(solution)/shard_map/ppermute | solution.py:226
  55.5 14.1 %collective-permute-start.13 = (bf16[1024,128]{1,0:T(8,128)(2,1)S(1)}, bf16[1024,128]{1,0:T(8,128)(2,1)S(1)}, u32[]{:S(2)}, u32[]{:S(2)}) collective-permute-start(bf16[1024,128]{1,0:T(8,128)(2,1)S(1)} %collective-permute-done.12.refs_2_), channel_id=1, source_target_pairs={{0,2},{1,3},{2,0},{3,1},{4,6},{5,7},{6,4},{7,5},{8,10},{9,11},{10,... | collective-permute-start | bytes 786440 | tf_op jit(solution)/shard_map/ppermute | solution.py:226
  66.2 4.9 %collective-permute-start.20 = (bf16[2048,128]{1,0:T(8,128)(2,1)S(1)}, bf16[2048,128]{1,0:T(8,128)(2,1)S(1)}, u32[]{:S(2)}, u32[]{:S(2)}) collective-permute-start(bf16[2048,128]{1,0:T(8,128)(2,1)S(1)} %collective-permute-done.14.refs_4_), channel_id=1, source_target_pairs={{0,1},{1,0},{2,3},{3,2},{4,5},{5,4},{6,7},{7,6},{8,9},{9,8},{10,11... | collective-permute-start | bytes 1572872 | tf_op jit(solution)/shard_map/ppermute | solution.py:226
  66.2 4.9 %collective-permute-start.21 = (bf16[2048,128]{1,0:T(8,128)(2,1)S(1)}, bf16[2048,128]{1,0:T(8,128)(2,1)S(1)}, u32[]{:S(2)}, u32[]{:S(2)}) collective-permute-start(bf16[2048,128]{1,0:T(8,128)(2,1)S(1)} %collective-permute-done.15.refs_5_), channel_id=1, source_target_pairs={{0,1},{1,0},{2,3},{3,2},{4,5},{5,4},{6,7},{7,6},{8,9},{9,8},{10,11... | collective-permute-start | bytes 1572872 | tf_op jit(solution)/shard_map/ppermute | solution.py:226
  66.8 2.9 %collective-permute-start.17 = (bf16[1024,128]{1,0:T(8,128)(2,1)S(1)}, bf16[1024,128]{1,0:T(8,128)(2,1)S(1)}, u32[]{:S(2)}, u32[]{:S(2)}) collective-permute-start(bf16[1024,128]{1,0:T(8,128)(2,1)S(1)} %collective-permute-done.10.refs_1_), channel_id=1, source_target_pairs={{0,1},{1,0},{2,3},{3,2},{4,5},{5,4},{6,7},{7,6},{8,9},{9,8},{10,11... | collective-permute-start | bytes 786440 | tf_op jit(solution)/shard_map/ppermute | solution.py:226
  66.8 2.9 %collective-permute-start.18 = (bf16[1024,128]{1,0:T(8,128)(2,1)S(1)}, bf16[1024,128]{1,0:T(8,128)(2,1)S(1)}, u32[]{:S(2)}, u32[]{:S(2)}) collective-permute-start(bf16[1024,128]{1,0:T(8,128)(2,1)S(1)} %collective-permute-done.12.refs_2_), channel_id=1, source_target_pairs={{0,1},{1,0},{2,3},{3,2},{4,5},{5,4},{6,7},{7,6},{8,9},{9,8},{10,11... | collective-permute-start | bytes 786440 | tf_op jit(solution)/shard_map/ppermute | solution.py:226
  69.6 1.5 collective-permute-start.19
  73.5 35.9 %all-to-all-start.1 = ((bf16[16,256,128]{2,1,0:T(8,128)(2,1)}), bf16[16,256,128]{2,1,0:T(8,128)(2,1)}, u32[]{:S(2)}, u32[]{:S(2)}) async-start(bf16[16,256,128]{2,1,0:T(8,128)(2,1)} %shard_map.96), calls=%async_computation.1 | async-start | bytes 2097152 | tf_op jit(solution)/shard_map/all_to_all | solution.py:288
  82.0 1.4 copy-start.20
  82.0 5.0 %collective-permute-start.23 = (s32[2,32]{1,0:T(2,128)S(1)}, s32[2,32]{1,0:T(2,128)S(1)}, u32[]{:S(2)}, u32[]{:S(2)}) collective-permute-start(s32[2,32]{1,0:T(2,128)S(1)} %pad_add_fusion), channel_id=1, source_target_pairs={{0,1},{1,0},{2,3},{3,2},{4,5},{5,4},{6,7},{7,6},{8,9},{9,8},{10,11... | collective-permute-start | bytes 776 | tf_op jit(solution)/shard_map/ppermute | solution.py:226
  82.8 5.8 %collective-permute-start.22 = (bf16[32,128,128]{2,1,0:T(8,128)(2,1)S(1)}, bf16[32,128,128]{2,1,0:T(8,128)(2,1)S(1)}, u32[]{:S(2)}, u32[]{:S(2)}) collective-permute-start(bf16[32,128,128]{2,1,0:T(8,128)(2,1)S(1)} %bitcast.37), channel_id=1, source_target_pairs={{0,1},{1,0},{2,3},{3,2},{4,5},{5,4},{6,7},{7,6},{8,9},{9,8},{10,11... | collective-permute-start | bytes 3145736 | tf_op jit(solution)/shard_map/ppermute | solution.py:226
  88.6 1.0 copy-start.1
  90.0 19.4 %copy-start.9 = (s32[32]{0:T(128)}, s32[32]{0:T(128)S(1)}, u32[]{:S(2)}) copy-start(s32[32]{0:T(128)S(1)} %reshape.524.refs_0_) | copy-start | bytes 388
  91.1 0.7 copy-start.5
  113.9 31.7 %all-to-all-start.2 = ((bf16[16,256,128]{2,1,0:T(8,128)(2,1)}), bf16[16,256,128]{2,1,0:T(8,128)(2,1)S(1)}, u32[]{:S(2)}, u32[]{:S(2)}) async-start(bf16[16,256,128]{2,1,0:T(8,128)(2,1)} %get-tuple-element.58), calls=%async_computation.2 | async-start | bytes 2097152 | tf_op jit(solution)/shard_map/all_to_all | solution.py:288
  122.4 1.4 collective-permute-start.30
  124.8 6.1 %collective-permute-start.31 = (f32[64,256]{1,0:T(8,128)S(1)}, f32[64,256]{1,0:T(8,128)S(1)}, u32[]{:S(2)}, u32[]{:S(2)}) collective-permute-start(f32[64,256]{1,0:T(8,128)S(1)} %constant_dynamic-slice_fusion.3), channel_id=1, source_target_pairs={{0,2},{1,3},{2,0},{3,1},{4,6},{5,7},{6,4},{7,5},{8,10},{9,11},{10,... | collective-permute-start | bytes 196616 | tf_op jit(solution)/shard_map/ppermute | solution.py:226
  131.0 3.8 %collective-permute-start.32 = (f32[16,256]{1,0:T(8,128)S(1)}, f32[16,256]{1,0:T(8,128)S(1)}, u32[]{:S(2)}, u32[]{:S(2)}) collective-permute-start(f32[16,256]{1,0:T(8,128)S(1)} %get-tuple-element.102), channel_id=1, source_target_pairs={{0,4},{1,5},{2,6},{3,7},{4,8},{5,9},{6,10},{7,11},{8,12},{9,13},{1... | collective-permute-start | bytes 49160 | tf_op jit(solution)/shard_map/ppermute | solution.py:226
  132.4 5.2 %collective-permute-start.33 = (f32[16,256]{1,0:T(8,128)S(1)}, f32[16,256]{1,0:T(8,128)S(1)}, u32[]{:S(2)}, u32[]{:S(2)}) collective-permute-start(f32[16,256]{1,0:T(8,128)S(1)} %get-tuple-element.100), channel_id=1, source_target_pairs={{0,8},{1,9},{2,10},{3,11},{4,12},{5,13},{6,14},{7,15},{8,0},{9,1},... | collective-permute-start | bytes 49160 | tf_op jit(solution)/shard_map/ppermute | solution.py:226
  133.6 4.9 %collective-permute-start.34 = (f32[16,256]{1,0:T(8,128)S(1)}, f32[16,256]{1,0:T(8,128)S(1)}, u32[]{:S(2)}, u32[]{:S(2)}) collective-permute-start(f32[16,256]{1,0:T(8,128)S(1)} %get-tuple-element.101), channel_id=1, source_target_pairs={{0,12},{1,13},{2,14},{3,15},{4,0},{5,1},{6,2},{7,3},{8,4},{9,5},{1... | collective-permute-start | bytes 49160 | tf_op jit(solution)/shard_map/ppermute | solution.py:226
  139.2 14.7 %copy-start.2 = (bf16[32,128,128]{2,1,0:T(8,128)(2,1)S(1)}, bf16[32,128,128]{2,1,0:T(8,128)(2,1)}, u32[]{:S(2)}) copy-start(bf16[32,128,128]{2,1,0:T(8,128)(2,1)} %copy-done.1) | copy-start | bytes 3145732
  145.6 1.0 copy-start.3
  146.5 34.4 %all-to-all-start.3 = ((bf16[16,288,128]{2,1,0:T(8,128)(2,1)}), bf16[16,288,128]{2,1,0:T(8,128)(2,1)S(1)}, u32[]{:S(2)}, u32[]{:S(2)}) async-start(bf16[16,288,128]{2,1,0:T(8,128)(2,1)} %broadcast_dynamic-update-slice_fusion), calls=%async_computation.3 | async-start | bytes 2359296 | tf_op jit(solution)/shard_map/all_to_all | solution.py:288
  151.0 3.0 %collective-permute-start.24 = (bf16[16,256,128]{2,1,0:T(8,128)(2,1)}, bf16[16,256,128]{2,1,0:T(8,128)(2,1)S(1)}, u32[]{:S(2)}, u32[]{:S(2)}) collective-permute-start(bf16[16,256,128]{2,1,0:T(8,128)(2,1)} %copy-done.3), channel_id=1, source_target_pairs={{0,1},{1,0},{2,3},{3,2},{4,5},{5,4},{6,7},{7,6},{8,9},{9,8},{10,11... | collective-permute-start | bytes 3145736 | tf_op jit(solution)/shard_map/ppermute | solution.py:226
  153.9 1.2 copy-start.4
  160.2 18.3 %collective-permute-start.25 = (bf16[2048,128]{1,0:T(8,128)(2,1)S(1)}, bf16[2048,128]{1,0:T(8,128)(2,1)S(1)}, u32[]{:S(2)}, u32[]{:S(2)}) collective-permute-start(bf16[2048,128]{1,0:T(8,128)(2,1)S(1)} %get-tuple-element.60), channel_id=1, source_target_pairs={{0,4},{1,5},{2,6},{3,7},{4,8},{5,9},{6,10},{7,11},{8,12},{9,13},{1... | collective-permute-start | bytes 1572872 | tf_op jit(solution)/shard_map/ppermute | solution.py:226
  161.5 17.0 %collective-permute-start.26 = (bf16[2048,128]{1,0:T(8,128)(2,1)S(1)}, bf16[2048,128]{1,0:T(8,128)(2,1)S(1)}, u32[]{:S(2)}, u32[]{:S(2)}) collective-permute-start(bf16[2048,128]{1,0:T(8,128)(2,1)S(1)} %get-tuple-element.61), channel_id=1, source_target_pairs={{0,12},{1,13},{2,14},{3,15},{4,0},{5,1},{6,2},{7,3},{8,4},{9,5},{1... | collective-permute-start | bytes 1572872 | tf_op jit(solution)/shard_map/ppermute | solution.py:226
  162.2 15.5 %collective-permute-start.28 = (bf16[1024,128]{1,0:T(8,128)(2,1)S(1)}, bf16[1024,128]{1,0:T(8,128)(2,1)S(1)}, u32[]{:S(2)}, u32[]{:S(2)}) collective-permute-start(bf16[1024,128]{1,0:T(8,128)(2,1)S(1)} %get-tuple-element.64), channel_id=1, source_target_pairs={{0,2},{1,3},{2,0},{3,1},{4,6},{5,7},{6,4},{7,5},{8,10},{9,11},{10,... | collective-permute-start | bytes 786440 | tf_op jit(solution)/shard_map/ppermute | solution.py:226
  180.9 3.7 %copy-start.11 = (s32[32]{0:T(128)S(1)}, s32[32]{0:T(128)}, u32[]{:S(2)}) copy-start(s32[32]{0:T(128)} %copy-done.10) | copy-start | bytes 388
  180.9 3.7 %copy-start.13 = (s32[32]{0:T(128)S(1)}, s32[32]{0:T(128)}, u32[]{:S(2)}) copy-start(s32[32]{0:T(128)} %copy-done.12) | copy-start | bytes 388
  181.0 3.6 %collective-permute-start.35 = (bf16[16,256,128]{2,1,0:T(8,128)(2,1)S(1)}, bf16[16,256,128]{2,1,0:T(8,128)(2,1)S(1)}, u32[]{:S(2)}, u32[]{:S(2)}) collective-permute-start(bf16[16,256,128]{2,1,0:T(8,128)(2,1)S(1)} %slice.93), channel_id=1, source_target_pairs={{0,1},{1,0},{2,3},{3,2},{4,5},{5,4},{6,7},{7,6},{8,9},{9,8},{10,11... | collective-permute-start | bytes 3145736 | tf_op jit(solution)/shard_map/ppermute | solution.py:226
  181.1 10.4 %collective-permute-start.29 = (bf16[1024,128]{1,0:T(8,128)(2,1)}, bf16[1024,128]{1,0:T(8,128)(2,1)S(1)}, u32[]{:S(2)}, u32[]{:S(2)}) collective-permute-start(bf16[1024,128]{1,0:T(8,128)(2,1)} %add_convert_fusion.5), channel_id=1, source_target_pairs={{0,8},{1,9},{2,10},{3,11},{4,12},{5,13},{6,14},{7,15},{8,0},{9,1},... | collective-permute-start | bytes 786440 | tf_op jit(solution)/shard_map/ppermute | solution.py:226
  182.2 10.1 %collective-permute-start.27 = (bf16[1024,128]{1,0:T(8,128)(2,1)}, bf16[1024,128]{1,0:T(8,128)(2,1)S(1)}, u32[]{:S(2)}, u32[]{:S(2)}) collective-permute-start(bf16[1024,128]{1,0:T(8,128)(2,1)} %get-tuple-element.96), channel_id=1, source_target_pairs={{0,2},{1,3},{2,0},{3,1},{4,6},{5,7},{6,4},{7,5},{8,10},{9,11},{10,... | collective-permute-start | bytes 786440 | tf_op jit(solution)/shard_map/ppermute | solution.py:226
  189.2 0.7 copy-start.6
  191.6 5.3 %copy-start.16 = (bf16[1024,128]{1,0:T(8,128)(2,1)}, bf16[1024,128]{1,0:T(8,128)(2,1)S(1)}, u32[]{:S(2)}) copy-start(bf16[1024,128]{1,0:T(8,128)(2,1)S(1)} %collective-permute-done.29) | copy-start | bytes 786436
  191.6 19.2 %copy-start.8 = (bf16[1024,128]{1,0:T(8,128)(2,1)S(1)}, bf16[1024,128]{1,0:T(8,128)(2,1)}, u32[]{:S(2)}) copy-start(bf16[1024,128]{1,0:T(8,128)(2,1)} %copy-done.7) | copy-start | bytes 786436
  192.3 4.5 %copy-start.18 = (bf16[1024,128]{1,0:T(8,128)(2,1)}, bf16[1024,128]{1,0:T(8,128)(2,1)S(1)}, u32[]{:S(2)}) copy-start(bf16[1024,128]{1,0:T(8,128)(2,1)S(1)} %collective-permute-done.27) | copy-start | bytes 786436
  192.3 13.4 %collective-permute-start.36 = (bf16[2048,128]{1,0:T(8,128)(2,1)}, bf16[2048,128]{1,0:T(8,128)(2,1)S(1)}, u32[]{:S(2)}, u32[]{:S(2)}) collective-permute-start(bf16[2048,128]{1,0:T(8,128)(2,1)} %get-tuple-element.77), channel_id=1, source_target_pairs={{0,4},{1,5},{2,6},{3,7},{4,8},{5,9},{6,10},{7,11},{8,12},{9,13},{1... | collective-permute-start | bytes 1572872 | tf_op jit(solution)/shard_map/ppermute | solution.py:226
  194.4 16.4 %collective-permute-start.37 = (bf16[2048,128]{1,0:T(8,128)(2,1)}, bf16[2048,128]{1,0:T(8,128)(2,1)S(1)}, u32[]{:S(2)}, u32[]{:S(2)}) collective-permute-start(bf16[2048,128]{1,0:T(8,128)(2,1)} %get-tuple-element.78), channel_id=1, source_target_pairs={{0,12},{1,13},{2,14},{3,15},{4,0},{5,1},{6,2},{7,3},{8,4},{9,5},{1... | collective-permute-start | bytes 1572872 | tf_op jit(solution)/shard_map/ppermute | solution.py:226
  194.4 9.8 %collective-permute-start.39 = (bf16[1024,128]{1,0:T(8,128)(2,1)}, bf16[1024,128]{1,0:T(8,128)(2,1)S(1)}, u32[]{:S(2)}, u32[]{:S(2)}) collective-permute-start(bf16[1024,128]{1,0:T(8,128)(2,1)} %get-tuple-element.81), channel_id=1, source_target_pairs={{0,2},{1,3},{2,0},{3,1},{4,6},{5,7},{6,4},{7,5},{8,10},{9,11},{10,... | collective-permute-start | bytes 786440 | tf_op jit(solution)/shard_map/ppermute | solution.py:226
  197.6 15.8 %all-to-all-start.4 = ((f32[16,32,128]{2,1,0:T(8,128)}), f32[16,32,128]{2,1,0:T(8,128)S(1)}, u32[]{:S(2)}, u32[]{:S(2)}) async-start(f32[16,32,128]{2,1,0:T(8,128)} %broadcast_in_dim.7), calls=%async_computation.4 | async-start | bytes 524288 | tf_op jit(solution)/shard_map/all_to_all | solution.py:438
  205.3 16.0 %copy-start.14 = (bf16[256,256]{1,0:T(8,128)(2,1)S(1)}, bf16[256,256]{1,0:T(8,128)(2,1)}, u32[]{:S(2)}) copy-start(bf16[256,256]{1,0:T(8,128)(2,1)} %refs_4_.1) | copy-start | bytes 393220
  210.9 8.0 %collective-permute-start.38 = (bf16[1024,128]{1,0:T(8,128)(2,1)S(1)}, bf16[1024,128]{1,0:T(8,128)(2,1)S(1)}, u32[]{:S(2)}, u32[]{:S(2)}) collective-permute-start(bf16[1024,128]{1,0:T(8,128)(2,1)S(1)} %add_convert_fusion.2), channel_id=1, source_target_pairs={{0,2},{1,3},{2,0},{3,1},{4,6},{5,7},{6,4},{7,5},{8,10},{9,11},{10,... | collective-permute-start | bytes 786440 | tf_op jit(solution)/shard_map/ppermute | solution.py:226
  213.4 7.9 %collective-permute-start.40 = (bf16[1024,128]{1,0:T(8,128)(2,1)S(1)}, bf16[1024,128]{1,0:T(8,128)(2,1)S(1)}, u32[]{:S(2)}, u32[]{:S(2)}) collective-permute-start(bf16[1024,128]{1,0:T(8,128)(2,1)S(1)} %add_convert_fusion.1), channel_id=1, source_target_pairs={{0,8},{1,9},{2,10},{3,11},{4,12},{5,13},{6,14},{7,15},{8,0},{9,1},... | collective-permute-start | bytes 786440 | tf_op jit(solution)/shard_map/ppermute | solution.py:226
  214.3 7.3 %copy-start.15 = (bf16[1024,128]{1,0:T(8,128)(2,1)S(1)}, bf16[1024,128]{1,0:T(8,128)(2,1)}, u32[]{:S(2)}) copy-start(bf16[1024,128]{1,0:T(8,128)(2,1)} %get-tuple-element.97) | copy-start | bytes 786436
  214.3 7.3 %copy-start.17 = (bf16[1024,128]{1,0:T(8,128)(2,1)S(1)}, bf16[1024,128]{1,0:T(8,128)(2,1)}, u32[]{:S(2)}) copy-start(bf16[1024,128]{1,0:T(8,128)(2,1)} %copy-done.16) | copy-start | bytes 786436
  214.3 7.3 %copy-start.19 = (bf16[1024,128]{1,0:T(8,128)(2,1)S(1)}, bf16[1024,128]{1,0:T(8,128)(2,1)}, u32[]{:S(2)}) copy-start(bf16[1024,128]{1,0:T(8,128)(2,1)} %copy-done.18) | copy-start | bytes 786436
  (3 other events, 1.7 us)
